TPU v7x, 128 devices: a whole 4x4x4 slice. The times are simulated.
128 devices in a mesh: dp: 1, ctx: 16 (over y, x), tp: 8 (over z, core).
Axes of the slice: x: 4, y: 4, z: 4, core: 2. Of those that a mesh axis runs over, the one named last changes fastest.
Arguments:
- tokens: bfloat16 [4096, 4096], P(('dp', 'ctx', 'tp')), may hold values from -400 to 400
- projection: bfloat16 [4096, 6144], P('ctx', 'tp'), may hold values from -0.09375 to 0.09375
- norm_gain: float32 [4096], replicated, may hold values from 0.5 to 1.5
- query_gain: float32 [128], replicated, may hold values from 0.1 to 1.9
- key_gain: float32 [128], replicated, may hold values from 0.1 to 1.9
- segment_ids: int32 [4096], P('dp'), may hold values from 0 to 15, never falling along the last dimension, each value on 1 to 3072 neighbouring positions
- context_cotangent: bfloat16 [4096, 4096], P(('dp', 'ctx'), 'tp'), may hold values from -48 to 48
Outputs:
- context: bfloat16 [4096, 4096], P(('dp', 'ctx'), 'tp')
- token_grads: float32 [4096, 4096], P(('dp', 'ctx', 'tp'))
- projection_grads: float32 [4096, 6144], P(('dp', 'ctx'), 'tp')
- norm_gain_grads: float32 [4096], P('dp')
- query_gain_grads: float32 [128], P('dp')
- key_gain_grads: float32 [128], P('dp')
Inputs may be any that keep to these rules, and one draw needn't show every extreme that they name: `segment_ids`: never falls along the document; each sub-document holds 1 to 3072 tokens, and one holds exactly that many.
All inputs are finite; a program needn't handle non-finite values.
Results may differ from a plain program's by a relative error of at most 0.02.
Values may be sent and summed in bfloat16 or wider, within the bound.
A program may use at most 128 MiB of HBM per device.

v0:
```python
import jax
import jax.numpy as jnp
from jax import lax
from jax.sharding import PartitionSpec as P

HEAD_WIDTH = 128
QUERY_PER_KEY = 4


EPSILON = 1e-06
THETA = 1000000.0


def rms_norm(values, gain):
    mean_square = jnp.mean(values * values, axis=-1, keepdims=True)
    return values * lax.rsqrt(mean_square + EPSILON) * gain


def rope_tables(positions, width):
    half = width // 2
    frequency = THETA ** (-2.0 * jnp.arange(half, dtype=jnp.float32) / width)
    angles = positions.astype(jnp.float32)[:, None] * frequency[None, :]
    return (jnp.cos(angles), jnp.sin(angles))


def rotate(values, cosine, sine):
    half = values.shape[-1] // 2
    layout = (cosine.shape[0],) + (1,) * (values.ndim - 2) + (half,)
    cosine = cosine.reshape(layout)
    sine = sine.reshape(layout)
    first = values[..., :half]
    second = values[..., half:]
    return jnp.concatenate(
        [first * cosine - second * sine, second * cosine + first * sine], axis=-1
    )


def masked_scores(queries, key_piece, query_segments, key_segments, scale):
    scores = (
        jnp.einsum("tkgd,skd->kgts", queries, key_piece, preferred_element_type=jnp.float32) * scale
    )
    same_segment = query_segments[:, None] == key_segments[None, :]
    return jnp.where(same_segment[None, None], jnp.exp(scores), 0.0)


def on_device(tokens, projection, norm_gain, query_gain, key_gain, segment_ids, context_cotangent):
    tokens_wide = tokens.astype(jnp.float32)
    normed_own = rms_norm(tokens_wide, norm_gain).astype(jnp.bfloat16)
    normed_values = lax.all_gather(normed_own, "tp", axis=0, tiled=True)
    local_tokens = normed_values.shape[0]
    column_count = projection.shape[1]
    groups = column_count // ((QUERY_PER_KEY + 2) * HEAD_WIDTH)
    total_sum = local_tokens * lax.axis_size("ctx")
    offset = lax.axis_index("ctx") * local_tokens
    scale = HEAD_WIDTH ** (-0.5)
    joined_rows = jnp.dot(
        normed_values,
        lax.all_gather(projection, "ctx", axis=0, tiled=True),
        preferred_element_type=jnp.float32,
    )
    joined_rows = joined_rows.reshape(local_tokens, groups, QUERY_PER_KEY + 2, HEAD_WIDTH)
    query_raw = joined_rows[:, :, :QUERY_PER_KEY, :]
    key_raw = joined_rows[:, :, QUERY_PER_KEY, :]
    value_raw = joined_rows[:, :, QUERY_PER_KEY + 1, :]
    positions = offset + jnp.arange(local_tokens, dtype=jnp.int32)
    cosine, sine = rope_tables(positions, HEAD_WIDTH)

    def head_map(raw, gain):
        return rotate(rms_norm(raw, gain), cosine, sine)

    queries = head_map(query_raw, query_gain).astype(jnp.bfloat16)
    keys = head_map(key_raw, key_gain).astype(jnp.bfloat16)
    values = value_raw.astype(jnp.bfloat16)
    query_segments = lax.dynamic_slice_in_dim(segment_ids, offset, local_tokens)
    key_piece = lax.all_gather(keys, "ctx", axis=0, tiled=True)
    value_piece = lax.all_gather(values, "ctx", axis=0, tiled=True)
    key_segments = segment_ids
    exponent = masked_scores(queries, key_piece, query_segments, key_segments, scale)
    update = jnp.einsum(
        "kgts,skd->tkgd",
        exponent.astype(jnp.bfloat16),
        value_piece,
        preferred_element_type=jnp.float32,
    )
    denominator = jnp.sum(exponent, axis=-1)
    context = (update / jnp.transpose(denominator, (2, 0, 1))[..., None]).astype(jnp.bfloat16)
    upstream_gradient = context_cotangent.reshape(local_tokens, groups, QUERY_PER_KEY, HEAD_WIDTH)
    correction = jnp.transpose(
        jnp.sum(upstream_gradient.astype(jnp.float32) * context.astype(jnp.float32), axis=-1),
        (1, 2, 0),
    )
    keys_all, values_all = (
        lax.all_gather(keys, "ctx", axis=0, tiled=True),
        lax.all_gather(values, "ctx", axis=0, tiled=True),
    )
    block_rows = min(512, total_sum)

    def backward_block(running, index):
        start = index * block_rows
        key_block = lax.dynamic_slice_in_dim(keys_all, start, block_rows)
        value_block = lax.dynamic_slice_in_dim(values_all, start, block_rows)
        key_segments = lax.dynamic_slice_in_dim(segment_ids, start, block_rows)
        exponent = masked_scores(queries, key_block, query_segments, key_segments, scale)
        probabilities = exponent / denominator[..., None]
        prob_grads = jnp.einsum(
            "tkgd,skd->kgts", upstream_gradient, value_block, preferred_element_type=jnp.float32
        )
        score_grads = (probabilities * (prob_grads - correction[..., None])).astype(jnp.bfloat16)
        query_update = (
            jnp.einsum("kgts,skd->tkgd", score_grads, key_block, preferred_element_type=jnp.float32)
            * scale
        )
        key_update = (
            jnp.einsum("kgts,tkgd->skd", score_grads, queries, preferred_element_type=jnp.float32)
            * scale
        )
        value_update = jnp.einsum(
            "kgts,tkgd->skd",
            probabilities.astype(jnp.bfloat16),
            upstream_gradient,
            preferred_element_type=jnp.float32,
        )
        return (running + query_update, (key_update, value_update))

    query_grads, (key_blocks, value_blocks) = lax.scan(
        backward_block,
        jnp.zeros((local_tokens, groups, QUERY_PER_KEY, HEAD_WIDTH), jnp.float32),
        jnp.arange(total_sum // block_rows, dtype=jnp.int32),
    )
    key_grads_all = key_blocks.reshape(total_sum, groups, HEAD_WIDTH)
    value_grads_all = value_blocks.reshape(total_sum, groups, HEAD_WIDTH)
    key_grads, value_gradient = (
        lax.psum_scatter(
            key_grads_all.astype(jnp.bfloat16), "ctx", scatter_dimension=0, tiled=True
        ).astype(jnp.float32),
        lax.psum_scatter(
            value_grads_all.astype(jnp.bfloat16), "ctx", scatter_dimension=0, tiled=True
        ).astype(jnp.float32),
    )
    mapped, query_back = jax.vjp(head_map, query_raw, query_gain)
    unnormed_query_gradient, query_gain_term = query_back(query_grads)
    mapped, key_back = jax.vjp(head_map, key_raw, key_gain)
    unnormed_key_gradient, key_gain_term = key_back(key_grads)
    joined_gradient = (
        jnp.concatenate(
            [
                unnormed_query_gradient,
                unnormed_key_gradient[:, :, None, :],
                value_gradient[:, :, None, :],
            ],
            axis=2,
        )
        .reshape(local_tokens, column_count)
        .astype(jnp.bfloat16)
    )
    projection_grads = lax.psum_scatter(
        lax.dot_general(
            normed_values,
            joined_gradient,
            (((0,), (0,)), ((), ())),
            preferred_element_type=jnp.float32,
        ).astype(jnp.bfloat16),
        "ctx",
        scatter_dimension=0,
        tiled=True,
    ).astype(jnp.float32)
    normed_terms = lax.dot_general(
        joined_gradient,
        lax.all_gather(projection, "ctx", axis=0, tiled=True),
        (((1,), (1,)), ((), ())),
        preferred_element_type=jnp.float32,
    )
    normed_grads = lax.psum_scatter(
        normed_terms.astype(jnp.bfloat16), "tp", scatter_dimension=0, tiled=True
    ).astype(jnp.float32)
    mapped, norm_back = jax.vjp(rms_norm, tokens_wide, norm_gain)
    token_grads, norm_gain_term = norm_back(normed_grads)
    norm_gain_grads, query_gain_grads, key_gain_grads = lax.psum(
        (norm_gain_term, query_gain_term, key_gain_term), ("ctx", "tp")
    )
    return (
        context.reshape(local_tokens, groups * QUERY_PER_KEY * HEAD_WIDTH),
        token_grads,
        projection_grads,
        norm_gain_grads,
        query_gain_grads,
        key_gain_grads,
    )


def solution(mesh):
    placed = (
        P(("dp", "ctx", "tp"), None),
        P("ctx", "tp"),
        P(),
        P(),
        P(),
        P("dp"),
        P(("dp", "ctx"), "tp"),
    )
    return jax.shard_map(
        on_device,
        mesh=mesh,
        in_specs=placed,
        out_specs=(
            P(("dp", "ctx"), "tp"),
            P(("dp", "ctx", "tp"), None),
            P(("dp", "ctx"), "tp"),
            P("dp"),
            P("dp"),
            P("dp"),
        ),
        check_vma=False,
    )
```

profile of v0, /device:TPU:1, one launch (start us, length us, event | category | flops | bytes accessed | tf_op | source)
XLA Modules:
  0.0 579.2 jit_solution(14135531518084283991)
XLA Ops:
  7.2 1.1 fusion.52
  9.4 1.8 fusion.49
  12.1 28.3 %all-gather.6.cloned.1.call-done = bf16[256,4096]{1,0:T(8,128)(2,1)} async-done(((bf16[32,4096]{1,0:T(8,128)(2,1)}), bf16[256,4096]{1,0:T(8,128)(2,1)}) %all-gather.6.cloned.1.call-update) | async-done | bytes 2097168 | tf_op jit(solution)/shard_map/all_gather | solution.py:49
  40.3 63.3 %all-gather.8.cloned.1.call-done = bf16[4096,768]{1,0:T(8,128)(2,1)} async-done(((bf16[256,768]{1,0:T(8,128)(2,1)}), bf16[4096,768]{1,0:T(8,128)(2,1)}) %all-gather.8.cloned.1.call-update) | async-done | bytes 6291472 | tf_op jit(solution)/shard_map/all_gather | solution.py:58
  103.7 6.0 %fusion.82 = f32[256,768]{0,1:T(8,128)S(1)} fusion(bf16[256,4096]{1,0:T(8,128)(2,1)} %all-gather.6.cloned.1.call-done, bf16[4096,768]{1,0:T(8,128)(2,1)} %all-gather.8.cloned.1.call-done), kind=kOutput, calls=%fused_computation.122 | convolution fusion | flops 1610612736 | bytes 9175040 | tf_op jit(solution)/shard_map/dot_general | solution.py:56
  114.2 2.5 broadcast_compare_fusion.1
  117.6 1.2 slice.33
  120.6 32.9 %all-gather.10.cloned.1.call-done = bf16[4096,1,128]{2,0,1:T(8,128)(2,1)} async-done(((bf16[256,1,128]{2,0,1:T(8,128)(2,1)}), bf16[4096,1,128]{2,0,1:T(8,128)(2,1)}) %all-gather.10.cloned.1.call-update) | async-done | bytes 1048592 | tf_op jit(solution)/shard_map/all_gather | solution.py:75
  153.5 9.4 %fusion.25 = (f32[4,256]{1,0:T(4,128)}, f32[4096,256,4]{1,0,2:T(8,128)}) fusion(pred[256,4096]{0,1:T(8,128)(4,1)S(1)} %broadcast_compare_fusion.1, bf16[256,4,64]{2,0,1:T(8,128)(2,1)S(1)} %bitcast.226, bf16[256,4,64]{2,0,1:T(8,128)(2,1)S(1)} %bitcast.225, bf16[4096,1,128]{2,0,1:T(8,128)(2,1)} %all-gather.10.cloned.1.call-done), kind=kOutput, calls=%fused_computation.32 | convolution fusion | flops 1086848000 | bytes 19140608 | tf_op jit(solution)/shard_map/tkgd,skd->kgts/dot_general | solution.py:40
  163.0 35.1 %all-gather.12.cloned.1.call-done = bf16[4096,1,1,128]{0,3,2,1:T(8,128)(2,1)} async-done(((bf16[256,1,1,128]{0,3,2,1:T(8,128)(2,1)}), bf16[4096,1,1,128]{0,3,2,1:T(8,128)(2,1)}) %all-gather.12.cloned.1.call-update) | async-done | bytes 1048592 | tf_op jit(solution)/shard_map/all_gather | solution.py:76
  198.1 9.8 %multiply_reduce_fusion.2 = (f32[256,4]{0,1:T(4,128)S(1)}, bf16[256,1,4,128]{0,3,2,1:T(8,128)(2,1)}) fusion(bf16[256,1,4,128]{0,3,2,1:T(8,128)(2,1)S(1)} %bitcast.229, f32[256,4]{0,1:T(4,128)} %bitcast.15, f32[4096,256,4]{1,0,2:T(8,128)} %get-tuple-element.204, pred[256,4096]{0,1:T(8,128)(4,1)S(1)} %broadcast_compare_fusion.1, ...), kind=kOutput, calls=%fused_computation.66 | convolution fusion | flops 1087110144 | bytes 19406848 | tf_op jit(solution)/shard_map/kgts,skd->tkgd/dot_general | solution.py:79
  208.3 89.6 %while.15 = (s32[]{:T(128)}, f32[256,1,4,128]{0,3,2,1:T(8,128)}, bf16[8,512,1,128]{3,1,2,0:T(8,128)(2,1)}, bf16[8,512,1,128]{3,1,2,0:T(8,128)(2,1)}, s32[8]{0:T(...) while((s32[]{:T(128)}, f32[256,1,4,128]{0,3,2,1:T(8,128)}, ...), condition=%wide.region_6.7_spmd.clone, body=%wide.region_5.6_spmd.clone.sunk | while | flops 675348480 | bytes 12730609 | solution.py:125
  208.3 1.3 dynamic_slice.41
  211.2 1.6 fusion.116
  212.8 1.4 fusion.117
  214.2 2.1 fusion.119
  216.3 2.0 fusion.118
  219.4 1.3 dynamic_slice.41
  222.2 1.6 fusion.116
  223.9 1.4 fusion.117
  225.2 2.1 fusion.119
  227.3 2.2 fusion.118
  230.6 1.3 dynamic_slice.41
  233.5 1.6 fusion.116
  235.1 1.4 fusion.117
  236.5 2.0 fusion.119
  238.5 2.2 fusion.118
  241.8 1.3 dynamic_slice.41
  244.7 1.6 fusion.116
  246.3 1.4 fusion.117
  247.7 2.1 fusion.119
  249.8 2.2 fusion.118
  253.1 1.3 dynamic_slice.41
  255.9 1.6 fusion.116
  257.6 1.4 fusion.117
  258.9 2.0 fusion.119
  261.0 2.2 fusion.118
  264.3 1.3 dynamic_slice.41
  267.2 1.6 fusion.116
  268.8 1.4 fusion.117
  270.2 2.0 fusion.119
  272.2 2.2 fusion.118
  275.6 1.3 dynamic_slice.41
  278.4 1.6 fusion.116
  280.0 1.4 fusion.117
  281.4 2.0 fusion.119
  283.4 2.2 fusion.118
  286.8 1.3 dynamic_slice.41
  289.6 1.6 fusion.116
  291.2 1.4 fusion.117
  292.6 2.0 fusion.119
  294.7 2.2 fusion.118
  298.9 1.2 copy.34
  300.1 1.2 multiply_add_fusion.1
  302.4 67.8 %reduce-scatter.5.cloned.1.call-done = bf16[256,1,128]{2,0,1:T(8,128)(2,1)} async-done(((bf16[4096,1,128]{2,0,1:T(8,128)(2,1)}), bf16[256,1,128]{2,0,1:T(8,128)(2,1)}) %reduce-scatter.5.cloned.1.call-update) | async-done | bytes 65552 | tf_op jit(solution)/shard_map/reduce_scatter | solution.py:133
  372.1 73.7 %reduce-scatter.7.cloned.1.call-done = bf16[256,1,128]{2,0,1:T(8,128)(2,1)} async-done(((bf16[4096,1,128]{2,0,1:T(8,128)(2,1)}), bf16[256,1,128]{2,0,1:T(8,128)(2,1)}) %reduce-scatter.7.cloned.1.call-update) | async-done | bytes 65552 | tf_op jit(solution)/shard_map/reduce_scatter | solution.py:136
  446.8 6.1 %convolution_convert_fusion.1 = bf16[256,4096]{1,0:T(8,128)(2,1)} fusion(bf16[256,768]{0,1:T(8,128)(2,1)S(1)} %bitcast.223, bf16[4096,768]{1,0:T(8,128)(2,1)} %all-gather.8.cloned.1.call-done), kind=kOutput, calls=%fused_computation.38 | convolution fusion | flops 1611661312 | bytes 8781824 | tf_op jit(solution)/shard_map/dot_general | solution.py:167
  453.1 4.5 convolution_convert_fusion
  459.4 25.5 %reduce-scatter.9.cloned.1.call-done = bf16[32,4096]{1,0:T(8,128)(2,1)} async-done(((bf16[256,4096]{1,0:T(8,128)(2,1)}), bf16[32,4096]{1,0:T(8,128)(2,1)}) %reduce-scatter.9.cloned.1.call-update) | async-done | bytes 262160 | tf_op jit(solution)/shard_map/reduce_scatter | solution.py:173
  484.9 1.3 fusion.50
  486.2 68.6 %all-reduce.4 = (f32[4096]{0:T(1024)}, f32[128]{0:T(128)}, f32[128]{0:T(128)}) all-reduce(f32[4096]{0:T(1024)S(1)} %get-tuple-element.160, f32[128]{0:T(128)S(1)} %get-tuple-element.158, f32[128]{0:T(128)S(1)} %get-tuple-element.162), channel_id=1, replica_groups=mesh['dp'=1,'ctx'=16,'tp'=8] {'ctx','tp'}, use_global_device_ids=true, to_apply=%region_15.16 | all-reduce | flops 4352 | bytes 34816 | tf_op jit(solution)/shard_map/psum | solution.py:178
  554.8 1.9 add_add_fusion
  556.7 13.7 %reduce-scatter.11.cloned.1.call-done = bf16[256,768]{1,0:T(8,128)(2,1)} async-done(((bf16[4096,768]{1,0:T(8,128)(2,1)}), bf16[256,768]{1,0:T(8,128)(2,1)}) %reduce-scatter.11.cloned.1.call-update) | async-done | bytes 393232 | tf_op jit(solution)/shard_map/reduce_scatter | solution.py:156
  570.4 1.9 convert_element_type.135
  (129 shorter events, 32.0 us)
Async XLA Ops:
  7.2 33.2 %all-gather.6.cloned.1.call-start = ((), (), s32[]{:S(2)}) async-start(), calls=%async_computation.4 | async-start | bytes 2359296 | tf_op jit(solution)/shard_map/all_gather | solution.py:49
  8.3 0.5 copy-start.24
  8.8 0.5 copy-start.16
  11.2 92.5 %all-gather.8.cloned.1.call-start = ((), (), s32[]{:S(2)}) async-start(), calls=%async_computation.5 | async-start | bytes 6684672 | tf_op jit(solution)/shard_map/all_gather | solution.py:58
  11.9 141.6 %all-gather.10.cloned.1.call-start = ((), (), s32[]{:S(2)}) async-start(), calls=%async_computation.6 | async-start | bytes 1114112 | tf_op jit(solution)/shard_map/all_gather | solution.py:75
  12.0 105.1 %copy-start.18 = (f32[64]{0:T(128)}, f32[64]{0:T(128)S(1)}, u32[]{:S(2)}) copy-start(f32[64]{0:T(128)S(1)} %multiply_power_fusion) | copy-start | bytes 772
  12.0 105.1 %copy-start.12 = (f32[256]{0:T(256)}, f32[256]{0:T(256)S(1)}, u32[]{:S(2)}) copy-start(f32[256]{0:T(256)S(1)} %add_convert_fusion.1) | copy-start | bytes 3076
  12.0 99.0 %copy-start.20 = (f32[128]{0:T(128)S(1)}, f32[128]{0:T(128)}, u32[]{:S(2)}) copy-start(f32[128]{0:T(128)} %param.13) | copy-start | bytes 1540
  12.0 104.7 %copy-start.7 = (bf16[256,512]{1,0:T(8,128)(2,1)S(1)}, bf16[256,512]{1,0:T(8,128)(2,1)}, u32[]{:S(2)}) copy-start(bf16[256,512]{1,0:T(8,128)(2,1)} %param.15) | copy-start | bytes 786436
  109.7 7.2 %copy-start.6 = (f32[256,768]{0,1:T(8,128)}, f32[256,768]{0,1:T(8,128)S(1)}, u32[]{:S(2)}) copy-start(f32[256,768]{0,1:T(8,128)S(1)} %fusion.82) | copy-start | bytes 2359300
  109.7 9.6 %copy-start.22 = (f32[128]{0:T(128)S(1)}, f32[128]{0:T(128)}, u32[]{:S(2)}) copy-start(f32[128]{0:T(128)} %param.12) | copy-start | bytes 1540
  109.9 0.6 copy-start.14
  110.5 0.6 copy-start.10
  112.5 85.6 %all-gather.12.cloned.1.call-start = ((), (), s32[]{:S(2)}) async-start(), calls=%async_computation.11 | async-start | bytes 1114112 | tf_op jit(solution)/shard_map/all_gather | solution.py:76
  114.0 256.2 %reduce-scatter.5.cloned.1.call-start = ((), (), s32[]{:S(2)}) async-start(), calls=%async_computation.7 | async-start | bytes 1114112 | tf_op jit(solution)/shard_map/reduce_scatter | solution.py:133
  117.6 45.3 %copy-start.4 = (f32[256,64]{1,0:T(8,128)}, f32[256,64]{1,0:T(8,128)S(1)}, u32[]{:S(2)}) copy-start(f32[256,64]{1,0:T(8,128)S(1)} %get-tuple-element.201) | copy-start | bytes 196612
  117.6 45.3 %copy-start.5 = (f32[256,64]{1,0:T(8,128)}, f32[256,64]{1,0:T(8,128)S(1)}, u32[]{:S(2)}) copy-start(f32[256,64]{1,0:T(8,128)S(1)} %get-tuple-element.202) | copy-start | bytes 196612
  119.0 43.9 %copy-start = (f32[256,1,4,128]{3,0,2,1:T(8,128)}, f32[256,1,4,128]{3,0,2,1:T(8,128)S(1)}, u32[]{:S(2)}) copy-start(f32[256,1,4,128]{3,0,2,1:T(8,128)S(1)} %copy.45) | copy-start | bytes 1572868
  298.0 3.3 copy-start.1
  298.0 3.3 copy-start.23
  298.0 73.0 %copy-start.13 = (f32[256]{0:T(256)S(1)}, f32[256]{0:T(256)}, u32[]{:S(2)}) copy-start(f32[256]{0:T(256)} %copy-done.12) | copy-start | bytes 3076
  298.0 73.0 %copy-start.19 = (f32[64]{0:T(128)S(1)}, f32[64]{0:T(128)}, u32[]{:S(2)}) copy-start(f32[64]{0:T(128)} %copy-done.18) | copy-start | bytes 772
  298.0 147.7 %reduce-scatter.7.cloned.1.call-start = ((), (), s32[]{:S(2)}) async-start(), calls=%async_computation.8 | async-start | bytes 1114112 | tf_op jit(solution)/shard_map/reduce_scatter | solution.py:136
  298.1 73.6 %copy-start.11 = (f32[256]{0:T(256)S(1)}, f32[256]{0:T(256)}, u32[]{:S(2)}) copy-start(f32[256]{0:T(256)} %copy-done.10) | copy-start | bytes 3076
  298.1 73.6 %copy-start.21 = (f32[128]{0:T(128)S(1)}, f32[128]{0:T(128)}, u32[]{:S(2)}) copy-start(f32[128]{0:T(128)} %param.13) | copy-start | bytes 1540
  298.6 73.3 %copy-start.15 = (f32[256]{0:T(256)S(1)}, f32[256]{0:T(256)}, u32[]{:S(2)}) copy-start(f32[256]{0:T(256)} %copy-done.14) | copy-start | bytes 3076
  298.6 186.3 %reduce-scatter.9.cloned.1.call-start = ((), (), s32[]{:S(2)}) async-start(), calls=%async_computation.9 | async-start | bytes 2359296 | tf_op jit(solution)/shard_map/reduce_scatter | solution.py:173
  446.8 6.2 %copy-start.2 = (bf16[256,4096]{1,0:T(8,128)(2,1)S(1)}, bf16[256,4096]{1,0:T(8,128)(2,1)}, u32[]{:S(2)}) copy-start(bf16[256,4096]{1,0:T(8,128)(2,1)} %all-gather.6.cloned.1.call-done) | copy-start | bytes 6291460
  453.0 117.4 %reduce-scatter.11.cloned.1.call-start = ((), (), s32[]{:S(2)}) async-start(), calls=%async_computation.10 | async-start | bytes 6684672 | tf_op jit(solution)/shard_map/reduce_scatter | solution.py:156
  457.6 0.9 copy-start.8
  457.6 27.3 %copy-start.3 = (bf16[32,4096]{1,0:T(8,128)(2,1)S(1)}, bf16[32,4096]{1,0:T(8,128)(2,1)}, u32[]{:S(2)}) copy-start(bf16[32,4096]{1,0:T(8,128)(2,1)} %param.9) | copy-start | bytes 786436
  457.6 27.3 %copy-start.9 = (f32[4096]{0:T(1024)S(1)}, f32[4096]{0:T(1024)}, u32[]{:S(2)}) copy-start(f32[4096]{0:T(1024)} %param.11) | copy-start | bytes 49156
  457.6 27.3 %copy-start.17 = (f32[32]{0:T(128)S(1)}, f32[32]{0:T(128)}, u32[]{:S(2)}) copy-start(f32[32]{0:T(128)} %copy-done.16) | copy-start | bytes 388
  457.6 97.2 %copy-start.25 = (f32[32]{0:T(128)S(1)}, f32[32]{0:T(128)}, u32[]{:S(2)}) copy-start(f32[32]{0:T(128)} %copy-done.24) | copy-start | bytes 388
Sparse Core Ops, SparseCore 0:
  11.3 29.0 all-gather.5
  42.5 61.1 all-gather.7
  112.6 40.8 all-gather.9
  155.5 42.5 all-gather.11
  298.1 72.0 reduce-scatter.4
  373.6 72.1 reduce-scatter.6
  453.1 31.7 reduce-scatter.8
  488.3 82.0 reduce-scatter.10
where the time goes:
time: 581 us; the launch traced here: 579 us
  waiting for transfers between devices  342 us (59%)
  matrix products  102 us (18%)
  blocking collectives  68.6 us (12%)
  local copies, waits for them, and re-layouts  25.6 us (4%)
  other arithmetic  20.1 us (3%)
  between operations  14.6 us (3%)
    reduce_scatter x1, waiting for transfers between devices, on_device(): lax.psum_scatter(value_grads_all.astype(jnp.bfloat16), 'ctx', scatter_dim...  73.7 us
    psum x1, blocking collectives, on_device(): lax.psum((norm_gain_term, query_gain_term, key_gain_term), ('ctx', 'tp'))  68.6 us
    reduce_scatter x1, waiting for transfers between devices, on_device(): lax.psum_scatter(key_grads_all.astype(jnp.bfloat16), 'ctx', scatter_dimen...  67.8 us
    all_gather x1, waiting for transfers between devices, on_device(): lax.all_gather(projection, 'ctx', axis=0, tiled=True)  63.3 us
    all_gather x1, waiting for transfers between devices, on_device(): value_piece = lax.all_gather(values, 'ctx', axis=0, tiled=True)  35.1 us
    all_gather x1, waiting for transfers between devices, on_device(): key_piece = lax.all_gather(keys, 'ctx', axis=0, tiled=True)  32.9 us
    all_gather x1, waiting for transfers between devices, on_device(): normed_values = lax.all_gather(normed_own, 'tp', axis=0, tiled=True)  28.3 us
    reduce_scatter x1, waiting for transfers between devices, on_device(): lax.psum_scatter(normed_terms.astype(jnp.bfloat16), 'tp', scatter_dimensi...  25.5 us
  transfers between devices with their start and end apart: 8, of which 8 were waited for; matrix products, arithmetic and copies ran while one was open for 5% of the time, Pallas kernels for 0%

commit v1 on v0

v1 whole, which is shorter than its diff:
```python
import jax
import jax.numpy as jnp
from jax import lax
from jax.experimental import pallas as pl
from jax.experimental.pallas import tpu as pltpu
from jax.sharding import PartitionSpec as P

HEAD_WIDTH = 128
QUERY_PER_KEY = 4
KEY_BLOCK = 256
LOG2E = 1.4426950408889634
NT = (((1,), (1,)), ((), ()))


EPSILON = 1e-06
THETA = 1000000.0


def rms_norm(values, gain):
    mean_square = jnp.mean(values * values, axis=-1, keepdims=True)
    return values * lax.rsqrt(mean_square + EPSILON) * gain


def rope_tables(positions, width):
    half = width // 2
    frequency = THETA ** (-2.0 * jnp.arange(half, dtype=jnp.float32) / width)
    angles = positions.astype(jnp.float32)[:, None] * frequency[None, :]
    return (jnp.cos(angles), jnp.sin(angles))


def rotate(values, cosine, sine):
    half = values.shape[-1] // 2
    layout = (cosine.shape[0],) + (1,) * (values.ndim - 2) + (half,)
    cosine = cosine.reshape(layout)
    sine = sine.reshape(layout)
    first = values[..., :half]
    second = values[..., half:]
    return jnp.concatenate(
        [first * cosine - second * sine, second * cosine + first * sine], axis=-1
    )


def attention_kernel(
    span_ref, q_ref, kv_ref, up_ref, bound_ref,
    context_ref, dq_ref, dkv_ref,
    exp_ref, q4_ref, up4_ref, num_ref, den_ref, dqt_ref,
):
    rows = q_ref.shape[0]
    width = HEAD_WIDTH
    block = KEY_BLOCK
    scale = width ** (-0.5)
    start_row = bound_ref[0:1, :]
    end_row = bound_ref[1:2, :]
    low, high = span_ref[0], span_ref[1]
    for g in range(QUERY_PER_KEY):
        q4_ref[g] = q_ref[:, g * width : (g + 1) * width]
    num_ref[...] = jnp.zeros_like(num_ref)
    den_ref[...] = jnp.zeros_like(den_ref)
    dqt_ref[...] = jnp.zeros_like(dqt_ref)
    dkv_ref[...] = jnp.zeros_like(dkv_ref)

    def forward(i, carry):
        at = pl.ds(pl.multiple_of(i * block, block), block)
        key = kv_ref[at, 0:width]
        value_t = kv_ref[at, width : 2 * width].T
        place = lax.broadcasted_iota(jnp.int32, (block, rows), 0) + i * block
        mask = (place >= start_row) & (place < end_row)
        for g in range(QUERY_PER_KEY):
            scores = lax.dot_general(
                key, q4_ref[g], NT, preferred_element_type=jnp.float32
            )
            exponent = jnp.where(mask, jnp.exp2(scores * (scale * LOG2E)), 0.0)
            den_ref[g] += jnp.sum(exponent.reshape(block // 8, 8, rows), axis=0)
            rounded = exponent.astype(jnp.bfloat16)
            exp_ref[g, at, :] = rounded
            num_ref[g] += jnp.dot(value_t, rounded, preferred_element_type=jnp.float32)
        return carry

    lax.fori_loop(low, high, forward, 0)
    corrections = []
    for g in range(QUERY_PER_KEY):
        columns = slice(g * width, (g + 1) * width)
        inverse = 1.0 / jnp.sum(den_ref[g], axis=0, keepdims=True)
        context_t = (num_ref[g] * inverse).astype(jnp.bfloat16).astype(jnp.float32)
        context_ref[:, columns] = context_t.T.astype(jnp.bfloat16)
        up_t = up_ref[:, columns].astype(jnp.float32).T
        up_t = (up_t * inverse).astype(jnp.bfloat16).astype(jnp.float32)
        up4_ref[g] = up_t.T.astype(jnp.bfloat16)
        corrections.append(jnp.sum(up_t * context_t, axis=0, keepdims=True))

    def backward(i, carry):
        at = pl.ds(pl.multiple_of(i * block, block), block)
        key_t = kv_ref[at, 0:width].T
        value = kv_ref[at, width : 2 * width]
        dk = jnp.zeros((block, width), jnp.float32)
        dv = jnp.zeros((block, width), jnp.float32)
        for g in range(QUERY_PER_KEY):
            grads = lax.dot_general(
                value, up4_ref[g], NT, preferred_element_type=jnp.float32
            )
            rounded = exp_ref[g, at, :]
            ds = (rounded.astype(jnp.float32) * (grads - corrections[g])).astype(jnp.bfloat16)
            dk += jnp.dot(ds, q4_ref[g], preferred_element_type=jnp.float32)
            dv += jnp.dot(rounded, up4_ref[g], preferred_element_type=jnp.float32)
            dqt_ref[g] += jnp.dot(key_t, ds, preferred_element_type=jnp.float32)
        dkv_ref[at, 0:width] = (dk * scale).astype(jnp.bfloat16)
        dkv_ref[at, width : 2 * width] = dv.astype(jnp.bfloat16)
        return carry

    lax.fori_loop(low, high, backward, 0)
    for g in range(QUERY_PER_KEY):
        dq_ref[:, g * width : (g + 1) * width] = (dqt_ref[g] * scale).T


def attention(span, queries, keys_values, upstream, bounds):
    rows = queries.shape[0]
    total = keys_values.shape[0]
    group = QUERY_PER_KEY
    vmem = pl.BlockSpec(memory_space=pltpu.VMEM)
    return pl.pallas_call(
        attention_kernel,
        out_shape=(
            jax.ShapeDtypeStruct((rows, group * HEAD_WIDTH), jnp.bfloat16),
            jax.ShapeDtypeStruct((rows, group * HEAD_WIDTH), jnp.float32),
            jax.ShapeDtypeStruct((total, 2 * HEAD_WIDTH), jnp.bfloat16),
        ),
        in_specs=[pl.BlockSpec(memory_space=pltpu.SMEM)] + [vmem] * 4,
        out_specs=(vmem, vmem, vmem),
        scratch_shapes=[
            pltpu.VMEM((group, total, rows), jnp.bfloat16),
            pltpu.VMEM((group, rows, HEAD_WIDTH), jnp.bfloat16),
            pltpu.VMEM((group, rows, HEAD_WIDTH), jnp.bfloat16),
            pltpu.VMEM((group, HEAD_WIDTH, rows), jnp.float32),
            pltpu.VMEM((group, 8, rows), jnp.float32),
            pltpu.VMEM((group, HEAD_WIDTH, rows), jnp.float32),
        ],
        compiler_params=pltpu.CompilerParams(vmem_limit_bytes=48 * 1024 * 1024),
        cost_estimate=pl.CostEstimate(
            flops=14 * group * rows * total * HEAD_WIDTH,
            bytes_accessed=8 * total * HEAD_WIDTH,
            transcendentals=group * rows * total,
        ),
    )(span, queries, keys_values, upstream, bounds)


def on_device(tokens, projection, norm_gain, query_gain, key_gain, segment_ids, context_cotangent):
    tokens_wide = tokens.astype(jnp.float32)
    normed_own = rms_norm(tokens_wide, norm_gain).astype(jnp.bfloat16)
    normed_values = lax.all_gather(normed_own, "tp", axis=0, tiled=True)
    local_tokens = normed_values.shape[0]
    column_count = projection.shape[1]
    groups = column_count // ((QUERY_PER_KEY + 2) * HEAD_WIDTH)
    offset = lax.axis_index("ctx") * local_tokens
    joined_rows = jnp.dot(
        normed_values,
        lax.all_gather(projection, "ctx", axis=0, tiled=True),
        preferred_element_type=jnp.float32,
    )
    joined_rows = joined_rows.reshape(local_tokens, groups, QUERY_PER_KEY + 2, HEAD_WIDTH)
    query_raw = joined_rows[:, :, :QUERY_PER_KEY, :]
    key_raw = joined_rows[:, :, QUERY_PER_KEY, :]
    value_raw = joined_rows[:, :, QUERY_PER_KEY + 1, :]
    positions = offset + jnp.arange(local_tokens, dtype=jnp.int32)
    cosine, sine = rope_tables(positions, HEAD_WIDTH)

    def head_map(raw, gain):
        return rotate(rms_norm(raw, gain), cosine, sine)

    queries = head_map(query_raw, query_gain).astype(jnp.bfloat16)
    keys = head_map(key_raw, key_gain).astype(jnp.bfloat16)
    values = value_raw.astype(jnp.bfloat16)
    query_segments = lax.dynamic_slice_in_dim(segment_ids, offset, local_tokens)
    starts = jnp.sum((segment_ids[None, :] < query_segments[:, None]).astype(jnp.int32), axis=1)
    ends = jnp.sum((segment_ids[None, :] <= query_segments[:, None]).astype(jnp.int32), axis=1)
    bounds = jnp.stack([starts, ends])
    span = jnp.stack([starts[0] // KEY_BLOCK, (ends[-1] + KEY_BLOCK - 1) // KEY_BLOCK])
    keys_values = lax.all_gather(
        jnp.concatenate([keys[:, 0], values[:, 0]], axis=1), "ctx", axis=0, tiled=True
    )
    context, query_grads, kv_grads = attention(
        span,
        queries.reshape(local_tokens, -1),
        keys_values,
        context_cotangent,
        bounds,
    )
    query_grads = query_grads.reshape(local_tokens, groups, QUERY_PER_KEY, HEAD_WIDTH)
    kv_grads = lax.psum_scatter(kv_grads, "ctx", scatter_dimension=0, tiled=True).astype(jnp.float32)
    key_grads = kv_grads[:, None, :HEAD_WIDTH]
    value_gradient = kv_grads[:, None, HEAD_WIDTH:]
    mapped, query_back = jax.vjp(head_map, query_raw, query_gain)
    unnormed_query_gradient, query_gain_term = query_back(query_grads)
    mapped, key_back = jax.vjp(head_map, key_raw, key_gain)
    unnormed_key_gradient, key_gain_term = key_back(key_grads)
    joined_gradient = (
        jnp.concatenate(
            [
                unnormed_query_gradient,
                unnormed_key_gradient[:, :, None, :],
                value_gradient[:, :, None, :],
            ],
            axis=2,
        )
        .reshape(local_tokens, column_count)
        .astype(jnp.bfloat16)
    )
    projection_grads = lax.psum_scatter(
        lax.dot_general(
            normed_values,
            joined_gradient,
            (((0,), (0,)), ((), ())),
            preferred_element_type=jnp.float32,
        ).astype(jnp.bfloat16),
        "ctx",
        scatter_dimension=0,
        tiled=True,
    ).astype(jnp.float32)
    normed_terms = lax.dot_general(
        joined_gradient,
        lax.all_gather(projection, "ctx", axis=0, tiled=True),
        (((1,), (1,)), ((), ())),
        preferred_element_type=jnp.float32,
    )
    normed_grads = lax.psum_scatter(
        normed_terms.astype(jnp.bfloat16), "tp", scatter_dimension=0, tiled=True
    ).astype(jnp.float32)
    mapped, norm_back = jax.vjp(rms_norm, tokens_wide, norm_gain)
    token_grads, norm_gain_term = norm_back(normed_grads)
    norm_gain_grads, query_gain_grads, key_gain_grads = lax.psum(
        (norm_gain_term, query_gain_term, key_gain_term), ("ctx", "tp")
    )
    return (
        context.reshape(local_tokens, groups * QUERY_PER_KEY * HEAD_WIDTH),
        token_grads,
        projection_grads,
        norm_gain_grads,
        query_gain_grads,
        key_gain_grads,
    )


def solution(mesh):
    placed = (
        P(("dp", "ctx", "tp"), None),
        P("ctx", "tp"),
        P(),
        P(),
        P(),
        P("dp"),
        P(("dp", "ctx"), "tp"),
    )
    return jax.shard_map(
        on_device,
        mesh=mesh,
        in_specs=placed,
        out_specs=(
            P(("dp", "ctx"), "tp"),
            P(("dp", "ctx", "tp"), None),
            P(("dp", "ctx"), "tp"),
            P("dp"),
            P("dp"),
            P("dp"),
        ),
        check_vma=False,
    )
```

time: 581 us -> 398 us (0.69)
  matrix products: 102 us -> 16.7 us
  waiting for transfers between devices: 342 us -> 269 us
  local copies, waits for them, and re-layouts: 25.6 us -> 3.59 us
  Pallas kernels: 0 us -> 7.1 us
  other arithmetic: 20.1 us -> 13.6 us
    dot_general x42 -> x0, matrix products: 85.9 us -> none  [the longest x9 22.3 us: masked_scores(): jnp.einsum('tkgd,skd->kgts', queries, key_piece, preferred_element_type=j...]
    reduce_scatter x2 -> x1, waiting for transfers between devices: 142 us -> 98.2 us  [on_device(): lax.psum_scatter(kv_grads, 'ctx', scatter_dimension=0, tiled=True)]
    all_gather x2 -> x1, waiting for transfers between devices: 68 us -> 37.4 us  [on_device(): lax.all_gather(jnp.concatenate([keys[:, 0], values[:, 0]], axis=1), 'ctx'...]
    dynamic_slice x16 -> x0, local copies, waits for them, and re-layouts: 16.5 us -> none  [the longest x8 10.4 us: on_device(): lax.scan(backward_block, jnp.zeros((local_tokens, groups, QUERY_PER_KEY,...]
    pallas_call x0 -> x1, Pallas kernels: none -> 7.1 us  [attention(): pl.pallas_call(attention_kernel, out_shape=(jax.ShapeDtypeStruct((rows, g...]
  transfers between devices with their start and end apart: 8 -> 6, of which waited for: 8 -> 6; matrix products, arithmetic and copies ran while one was open for 5% -> 3% of each run, Pallas kernels for 0% -> 0%
where the time goes in v1:
time: 398 us; the launch traced here: 397 us
  waiting for transfers between devices  269 us (68%)
  blocking collectives  68.5 us (17%)
  between operations  17.7 us (4%)
  matrix products  16.7 us (4%)
  other arithmetic  13.6 us (3%)
  Pallas kernels  7.1 us (2%)
    reduce_scatter x1, waiting for transfers between devices, on_device(): lax.psum_scatter(kv_grads, 'ctx', scatter_dimension=0, tiled=True)  98.2 us
    psum x1, blocking collectives, on_device(): lax.psum((norm_gain_term, query_gain_term, key_gain_term), ('ctx', 'tp'))  68.5 us
    all_gather x1, waiting for transfers between devices, on_device(): lax.all_gather(projection, 'ctx', axis=0, tiled=True)  63.3 us
    all_gather x1, waiting for transfers between devices, on_device(): lax.all_gather(jnp.concatenate([keys[:, 0], values[:, 0]], axis=1), 'ctx'...  37.4 us
    all_gather x1, waiting for transfers between devices, on_device(): normed_values = lax.all_gather(normed_own, 'tp', axis=0, tiled=True)  28.3 us
    reduce_scatter x1, waiting for transfers between devices, on_device(): lax.psum_scatter(normed_terms.astype(jnp.bfloat16), 'tp', scatter_dimensi...  27 us
    reduce_scatter x1, waiting for transfers between devices, on_device(): lax.psum_scatter(lax.dot_general(normed_values, joined_gradient, (((0,),...  14.2 us
  transfers between devices with their start and end apart: 6, of which 6 were waited for; matrix products, arithmetic and copies ran while one was open for 3% of the time, Pallas kernels for 0%

profile of v1, /device:TPU:1, one launch (start us, length us, event | category | flops | bytes accessed | tf_op | source)
XLA Modules:
  0.0 396.9 jit_solution(6167602439993477743)
XLA Ops:
  7.2 0.0 all-gather.4.cloned.1.call-start
  7.2 1.1 fusion.5
  8.3 1.8 fusion.2
  10.1 0.0 all-gather.4.cloned.1.call-update
  10.1 0.0 all-gather.6.cloned.1.call-start
  10.2 0.7 all-gather.6.cloned.1.call-update
  10.9 0.0 all-gather.8.cloned.1.call-start
  11.0 0.0 copy-start.6
  11.0 0.0 copy-start.7
  11.0 0.0 copy-start.5
  11.0 28.3 %all-gather.4.cloned.1.call-done = bf16[256,4096]{1,0:T(8,128)(2,1)} async-done(((bf16[32,4096]{1,0:T(8,128)(2,1)}), bf16[256,4096]{1,0:T(8,128)(2,1)}) %all-gather.4.cloned.1.call-update) | async-done | bytes 2097168 | tf_op jit(solution)/shard_map/all_gather | solution.py:149
  39.3 63.3 %all-gather.6.cloned.1.call-done = bf16[4096,768]{1,0:T(8,128)(2,1)} async-done(((bf16[256,768]{1,0:T(8,128)(2,1)}), bf16[4096,768]{1,0:T(8,128)(2,1)}) %all-gather.6.cloned.1.call-update) | async-done | bytes 6291472 | tf_op jit(solution)/shard_map/all_gather | solution.py:156
  102.7 6.0 %fusion.32 = f32[256,768]{0,1:T(8,128)S(1)} fusion(bf16[256,4096]{1,0:T(8,128)(2,1)} %all-gather.4.cloned.1.call-done, bf16[4096,768]{1,0:T(8,128)(2,1)} %all-gather.6.cloned.1.call-done), kind=kOutput, calls=%fused_computation.80 | convolution fusion | flops 1610612736 | bytes 9175040 | tf_op jit(solution)/shard_map/dot_general | solution.py:154
  108.7 0.0 copy-start.1
  108.7 0.1 copy.29
  108.8 0.1 copy.28
  108.9 0.1 fusion.22
  109.1 0.0 copy-done.6
  109.1 0.1 fusion.24
  109.2 0.6 fusion.28
  109.8 0.8 pad_maximum_fusion.2
  110.5 0.0 all-gather.8.cloned.1.call-update
  110.5 0.0 reduce-scatter.4.cloned.1.call-start
  110.6 0.0 copy-done.7
  110.6 0.1 dynamic_slice.3
  110.7 1.0 convert_reduce_fusion.1
  111.7 0.6 slice.37
  113.0 0.5 slice.36
  116.1 0.1 pad_add_fusion.3.span_ref
  116.2 0.3 multiply_cosine_fusion.1
  116.5 0.1 multiply_reduce_fusion.2
  116.6 0.0 copy-done.5
  116.6 0.1 multiply_multiply_fusion
  116.7 0.1 subtract_convert_fusion
  116.8 0.1 copy.23.q_ref
  116.9 37.4 %all-gather.8.cloned.1.call-done.kv_ref = bf16[4096,256]{1,0:T(8,128)(2,1)} async-done(((bf16[256,256]{1,0:T(8,128)(2,1)}), bf16[4096,256]{1,0:T(8,128)(2,1)}) %all-gather.8.cloned.1.call-update) | async-done | bytes 2097168 | tf_op jit(solution)/shard_map/all_gather | solution.py:177
  154.4 0.0 copy-done.1
  154.4 1.6 copy-done
  156.0 7.1 %shard_map.118 = (bf16[256,512]{1,0:T(8,128)(2,1)}, f32[256,512]{1,0:T(8,128)S(1)}, bf16[4096,256]{1,0:T(8,128)(2,1)}) custom-call(s32[2]{0:T(128)S(1)} %pad_add_fusion.3.span_ref, bf16[256,512]{1,0:T(8,128)(2,1)S(1)} %copy.23.q_ref, bf16[4096,256]{1,0:T(8,128)(2,1)S(1)} %copy-done, bf16[256,512]{1,0:T(8,128)(2,1)S(1)} %copy-done.1, ...), custom_call_target="tpu_custom_call" | custom-call | flops 7516192768 | bytes 4194304 | tf_op jit(solution)/shard_map/pallas_call | solution.py:120
  163.1 0.0 reduce-scatter.4.cloned.1.call-update
  163.1 0.0 reduce-scatter.6.cloned.1.call-start
  163.1 0.2 copy.24
  163.3 0.1 multiply_add_fusion.1
  163.4 0.2 multiply_reduce_fusion
  163.6 0.2 fusion.4
  163.8 98.2 %reduce-scatter.4.cloned.1.call-done = bf16[256,256]{1,0:T(8,128)(2,1)} async-done(((bf16[4096,256]{1,0:T(8,128)(2,1)}), bf16[256,256]{1,0:T(8,128)(2,1)}) %reduce-scatter.4.cloned.1.call-update) | async-done | bytes 131088 | tf_op jit(solution)/shard_map/reduce_scatter | solution.py:188
  262.0 0.9 fusion.26
  262.9 0.1 copy.26
  263.0 0.6 fusion.19
  263.6 0.2 multiply_reduce_fusion.3
  263.8 0.2 fusion.25
  264.0 0.1 copy.25
  264.1 0.1 pad_maximum_fusion
  264.1 6.2 %convolution_convert_fusion.1 = bf16[256,4096]{1,0:T(8,128)(2,1)} fusion(bf16[256,768]{0,1:T(8,128)(2,1)S(1)} %bitcast.56, bf16[4096,768]{1,0:T(8,128)(2,1)} %all-gather.6.cloned.1.call-done), kind=kOutput, calls=%fused_computation.1 | convolution fusion | flops 1611661312 | bytes 8781824 | tf_op jit(solution)/shard_map/dot_general | solution.py:218
  270.3 0.0 reduce-scatter.6.cloned.1.call-update
  270.4 0.2 reduce-scatter.8.cloned.1.call-start
  270.6 4.5 %convolution_convert_fusion = bf16[4096,768]{1,0:T(8,128)(2,1)} fusion(bf16[256,4096]{1,0:T(8,128)(2,1)S(1)} %copy-done.2, bf16[256,768]{0,1:T(8,128)(2,1)S(1)} %bitcast.57), kind=kOutput, calls=%fused_computation | convolution fusion | flops 1613758464 | bytes 8781824 | tf_op jit(solution)/shard_map/dot_general | solution.py:208
  275.1 0.0 reduce-scatter.8.cloned.1.call-update
  275.2 27.0 %reduce-scatter.6.cloned.1.call-done = bf16[32,4096]{1,0:T(8,128)(2,1)} async-done(((bf16[256,4096]{1,0:T(8,128)(2,1)}), bf16[32,4096]{1,0:T(8,128)(2,1)}) %reduce-scatter.6.cloned.1.call-update) | async-done | bytes 262160 | tf_op jit(solution)/shard_map/reduce_scatter | solution.py:224
  302.2 1.3 fusion.3
  303.4 68.5 %all-reduce.4 = (f32[4096]{0:T(1024)}, f32[128]{0:T(128)}, f32[128]{0:T(128)}) all-reduce(f32[4096]{0:T(1024)S(1)} %get-tuple-element.14, f32[128]{0:T(128)S(1)} %get-tuple-element.12, f32[128]{0:T(128)S(1)} %get-tuple-element.16), channel_id=1, replica_groups=mesh['dp'=1,'ctx'=16,'tp'=8] {'ctx','tp'}, use_global_device_ids=true, to_apply=%region_12.13 | all-reduce | flops 4352 | bytes 34816 | tf_op jit(solution)/shard_map/psum | solution.py:229
  372.0 1.9 add_add_fusion
  373.9 14.2 %reduce-scatter.8.cloned.1.call-done = bf16[256,768]{1,0:T(8,128)(2,1)} async-done(((bf16[4096,768]{1,0:T(8,128)(2,1)}), bf16[256,768]{1,0:T(8,128)(2,1)}) %reduce-scatter.8.cloned.1.call-update) | async-done | bytes 393232 | tf_op jit(solution)/shard_map/reduce_scatter | solution.py:207
  388.1 1.9 convert_element_type.65
  (19 shorter events, 0.1 us)
Async XLA Ops:
  7.2 32.2 %all-gather.4.cloned.1.call-start = ((), (), s32[]{:S(2)}) async-start(), calls=%async_computation.3 | async-start | bytes 2359296 | tf_op jit(solution)/shard_map/all_gather | solution.py:149
  10.1 92.5 %all-gather.6.cloned.1.call-start = ((), (), s32[]{:S(2)}) async-start(), calls=%async_computation.4 | async-start | bytes 6684672 | tf_op jit(solution)/shard_map/all_gather | solution.py:156
  10.9 143.5 %all-gather.8.cloned.1.call-start = ((), (), s32[]{:S(2)}) async-start(), calls=%async_computation.5 | async-start | bytes 2228224 | tf_op jit(solution)/shard_map/all_gather | solution.py:177
  11.0 98.1 %copy-start.6 = (f32[128]{0:T(128)S(1)}, f32[128]{0:T(128)}, u32[]{:S(2)}) copy-start(f32[128]{0:T(128)} %param.11) | copy-start | bytes 1540
  11.0 99.6 %copy-start.7 = (s32[4096]{0:T(1024)S(1)}, s32[4096]{0:T(1024)}, u32[]{:S(2)}) copy-start(s32[4096]{0:T(1024)} %param.12) | copy-start | bytes 49156
  11.0 105.6 %copy-start.5 = (f32[128]{0:T(128)S(1)}, f32[128]{0:T(128)}, u32[]{:S(2)}) copy-start(f32[128]{0:T(128)} %param.10) | copy-start | bytes 1540
  108.7 45.7 %copy-start.1 = (bf16[256,512]{1,0:T(8,128)(2,1)S(1)}, bf16[256,512]{1,0:T(8,128)(2,1)}, u32[]{:S(2)}) copy-start(bf16[256,512]{1,0:T(8,128)(2,1)} %up_ref.1) | copy-start | bytes 786436
  110.5 151.4 %reduce-scatter.4.cloned.1.call-start = ((), (), s32[]{:S(2)}) async-start(), calls=%async_computation.6 | async-start | bytes 2228224 | tf_op jit(solution)/shard_map/reduce_scatter | solution.py:188
  154.4 1.6 copy-start
  163.1 139.1 %reduce-scatter.6.cloned.1.call-start = ((), (), s32[]{:S(2)}) async-start(), calls=%async_computation.7 | async-start | bytes 2359296 | tf_op jit(solution)/shard_map/reduce_scatter | solution.py:224
  264.1 6.4 %copy-start.2 = (bf16[256,4096]{1,0:T(8,128)(2,1)S(1)}, bf16[256,4096]{1,0:T(8,128)(2,1)}, u32[]{:S(2)}) copy-start(bf16[256,4096]{1,0:T(8,128)(2,1)} %all-gather.4.cloned.1.call-done) | copy-start | bytes 6291460
  270.4 117.8 %reduce-scatter.8.cloned.1.call-start = ((), (), s32[]{:S(2)}) async-start(), calls=%async_computation.8 | async-start | bytes 6684672 | tf_op jit(solution)/shard_map/reduce_scatter | solution.py:207
  275.1 27.0 %copy-start.3 = (bf16[32,4096]{1,0:T(8,128)(2,1)S(1)}, bf16[32,4096]{1,0:T(8,128)(2,1)}, u32[]{:S(2)}) copy-start(bf16[32,4096]{1,0:T(8,128)(2,1)} %param.7) | copy-start | bytes 786436
  275.1 27.0 %copy-start.4 = (f32[4096]{0:T(1024)S(1)}, f32[4096]{0:T(1024)}, u32[]{:S(2)}) copy-start(f32[4096]{0:T(1024)} %param.9) | copy-start | bytes 49156
Sparse Core Ops, SparseCore 0:
  10.3 28.9 all-gather.3
  41.5 61.1 all-gather.5
  110.7 43.6 all-gather.7
  163.2 98.7 reduce-scatter.3
  270.5 31.6 reduce-scatter.5
  305.8 82.2 reduce-scatter.7

commit v2 on v1

v2 whole, which is shorter than its diff:
```python
import jax
import jax.numpy as jnp
from jax import lax
from jax.experimental import pallas as pl
from jax.experimental.pallas import tpu as pltpu
from jax.sharding import PartitionSpec as P

HEAD_WIDTH = 128
QUERY_PER_KEY = 4
KEY_BLOCK = 256
SIDE = 4
EPSILON = 1e-06
THETA = 1000000.0
LOG2E = 1.4426950408889634
MESH = pl.DeviceIdType.MESH
NT = (((1,), (1,)), ((), ()))
TN = (((0,), (0,)), ((), ()))


def wrap(value):
    return lax.rem(value + 2 * SIDE, SIDE)


def part_of(step):
    return 0 if step == 1 else 1


class Torus:
    def __init__(self, send_sems, recv_sems):
        ctx, tp = lax.axis_index("ctx"), lax.axis_index("tp")
        self.place = {
            "y": lax.div(ctx, SIDE),
            "x": lax.rem(ctx, SIDE),
            "z": lax.div(tp, 2),
            "core": lax.rem(tp, 2),
        }
        self.tp = tp
        self.sems = (send_sems, recv_sems)
        self.sent = []

    def along(self, axis, step):
        at = self.place
        if axis == "x":
            return {"ctx": at["y"] * SIDE + wrap(at["x"] + step)}
        if axis == "y":
            return {"ctx": wrap(at["y"] + step) * SIDE + at["x"]}
        if axis == "z":
            return {"tp": wrap(at["z"] + step) * 2 + at["core"]}
        return {"tp": at["z"] * 2 + 1 - at["core"]}

    def greet(self, steps):
        barrier = pltpu.get_barrier_semaphore()
        partners = [(axis, step) for axis in ("x", "y", "z") for step in steps] + [("core", 1)]
        for axis, step in partners:
            pl.semaphore_signal(
                barrier, inc=1, device_id=self.along(axis, step), device_id_type=MESH
            )
        pl.semaphore_wait(barrier, len(partners))

    def copy(self, index, source, target, axis, step):
        return pltpu.make_async_remote_copy(
            src_ref=source,
            dst_ref=target,
            send_sem=self.sems[0].at[index],
            recv_sem=self.sems[1].at[index],
            device_id=self.along(axis, step),
            device_id_type=MESH,
        )

    def send(self, source, target, axis, step):
        index = len(self.sent)
        copy = self.copy(index, source, target, axis, step)
        copy.start()
        self.sent.append(copy)
        return index

    def arrive(self, index, target):
        self.copy(index, target, target, "core", 1).wait_recv()

    def close(self):
        for copy in self.sent:
            copy.wait_send()


class Blocks:
    def __init__(self, torus, data, orders):
        self.torus, self.data, self.orders = torus, data, orders
        self.rows = data.shape[0] // (SIDE * SIDE)
        self.keys = {}

    def at(self, half, first, second, part=None):
        offset = dict(zip(self.orders[half], (first, second)))
        place = self.torus.place
        block = wrap(place["y"] + offset["y"]) * SIDE + wrap(place["x"] + offset["x"])
        rows = self.rows
        start = block * rows + half * (rows // 2)
        if part is not None:
            start = start + part * (rows // 4)
        size = rows // 2 if part is None else rows // 4
        return self.data.at[pl.ds(pl.multiple_of(start, rows // 4), size), :]

    def send(self, key, source, target, axis, step):
        self.keys[key] = self.torus.send(source, target, axis, step)

    def arrive(self, key, target):
        self.torus.arrive(self.keys[key], target)


class Gather(Blocks):
    def __init__(self, torus, data):
        super().__init__(torus, data, (("x", "y"), ("y", "x")))

    def pass_on(self, half, first):
        for step in (1, -1):
            block = self.at(half, first, 0)
            self.send(("q", half, first, step), block, block, self.orders[half][1], step)

    def start(self):
        for half in (0, 1):
            for step in (1, -1):
                block = self.at(half, 0, 0)
                self.send(("p", half, step), block, block, self.orders[half][0], step)
        for half in (0, 1):
            self.pass_on(half, 0)

    def near(self):
        for half in (0, 1):
            for step in (1, -1):
                self.arrive(("p", half, step), self.at(half, -step, 0))
                block = self.at(half, -step, 0, part_of(step))
                self.send(("f", half, step), block, block, self.orders[half][0], step)
        for half in (0, 1):
            for step in (1, -1):
                self.pass_on(half, -step)

    def far(self):
        for half in (0, 1):
            for step in (1, -1):
                self.arrive(("f", half, step), self.at(half, 2, 0, part_of(step)))
            self.pass_on(half, 2)

    def cross(self, firsts):
        for first in firsts:
            for half in (0, 1):
                for step in (1, -1):
                    self.arrive(("q", half, first, step), self.at(half, first, -step))
                    block = self.at(half, first, -step, part_of(step))
                    self.send(("g", half, first, step), block, block, self.orders[half][1], step)

    def finish(self):
        for first in (0, -1, 1, 2):
            for half in (0, 1):
                for step in (1, -1):
                    self.arrive(("g", half, first, step), self.at(half, first, 2, part_of(step)))


def add_to(target, *sources):
    total = target[...].astype(jnp.float32)
    for source in sources:
        total = total + source[...].astype(jnp.float32)
    target[...] = total.astype(target.dtype)


class Scatter(Blocks):
    def __init__(self, torus, data, far_one, near_one, far_two, near_two):
        super().__init__(torus, data, (("y", "x"), ("x", "y")))
        self.far_one, self.near_one = far_one, near_one
        self.far_two, self.near_two = far_two, near_two

    def start(self, seconds=(2, 1, -1, 0)):
        for second in seconds:
            for half in (0, 1):
                for step in (1, -1):
                    self.send(
                        ("f1", half, second, step),
                        self.at(half, 2, second, part_of(step)),
                        self.far_one.at[half, second % SIDE, part_of(step)],
                        self.orders[half][0],
                        step,
                    )

    def turn(self, seconds=(2, 1, -1, 0)):
        for second in seconds:
            for half in (0, 1):
                for step in (1, -1):
                    landed = self.far_one.at[half, second % SIDE, part_of(step)]
                    self.arrive(("f1", half, second, step), landed)
                    add_to(self.at(half, step, second, part_of(step)), landed)
                    self.send(
                        ("n1", half, second, step),
                        self.at(half, step, second),
                        self.near_one.at[half, second % SIDE, part_of(step)],
                        self.orders[half][0],
                        step,
                    )

    def land(self, seconds=(2, 1, -1, 0)):
        for second in seconds:
            for half in (0, 1):
                landed = [self.near_one.at[half, second % SIDE, part] for part in (0, 1)]
                for step in (1, -1):
                    self.arrive(("n1", half, second, step), landed[part_of(step)])
                add_to(self.at(half, 0, second), *landed)
                if second == 2:
                    for step in (1, -1):
                        self.send(
                            ("f2", half, step),
                            self.at(half, 0, 2, part_of(step)),
                            self.far_two.at[half, part_of(step)],
                            self.orders[half][1],
                            step,
                        )

    def turn_two(self):
        for half in (0, 1):
            for step in (1, -1):
                landed = self.far_two.at[half, part_of(step)]
                self.arrive(("f2", half, step), landed)
                add_to(self.at(half, 0, step, part_of(step)), landed)
                self.send(
                    ("n2", half, step),
                    self.at(half, 0, step),
                    self.near_two.at[half, part_of(step)],
                    self.orders[half][1],
                    step,
                )

    def finish(self, store):
        for half in (0, 1):
            landed = [self.near_two.at[half, part] for part in (0, 1)]
            for step in (1, -1):
                self.arrive(("n2", half, step), landed[part_of(step)])
            total = self.at(half, 0, 0)[...].astype(jnp.float32)
            for source in landed:
                total = total + source[...].astype(jnp.float32)
            store(slice(half * (self.rows // 2), (half + 1) * (self.rows // 2)), total)


def scatter_scratch(rows, columns):
    return [
        pltpu.VMEM((2, SIDE, 2, rows // 4, columns), jnp.bfloat16),
        pltpu.VMEM((2, SIDE, 2, rows // 2, columns), jnp.bfloat16),
        pltpu.VMEM((2, 2, rows // 4, columns), jnp.bfloat16),
        pltpu.VMEM((2, 2, rows // 2, columns), jnp.bfloat16),
    ]


def inverse_rms(values):
    return lax.rsqrt(jnp.mean(values * values, axis=-1, keepdims=True) + EPSILON)


def turn_halves(values):
    return pltpu.roll(values, HEAD_WIDTH // 2, 1)


def head_map(raw, gain, cosine, sine):
    scaled = raw * inverse_rms(raw) * gain
    return scaled * cosine + turn_halves(scaled) * sine


def head_map_back(raw, gain, cosine, sine, grads):
    inverse = inverse_rms(raw)
    unit = raw * inverse
    turned = grads * cosine + turn_halves(grads * sine)
    gain_grads = jnp.sum(turned * unit, axis=0, keepdims=True)
    scaled = turned * gain
    raw_grads = inverse * (scaled - unit * jnp.mean(scaled * unit, axis=-1, keepdims=True))
    return raw_grads, gain_grads


def project_kernel(
    tokens_ref, shard_ref, norm_gain_ref, query_gain_ref, key_gain_ref, cosine_ref, sine_ref,
    q_ref, kv_ref, raw_ref, normed_ref, wkv_ref, wq_ref,
    send_sems, recv_sems,
):
    width = HEAD_WIDTH
    split = QUERY_PER_KEY * width
    torus = Torus(send_sems, recv_sems)
    torus.greet((1, -1))
    rows = shard_ref.shape[0]
    ctx = lax.axis_index("ctx")
    own = pl.ds(pl.multiple_of(ctx * rows, rows), rows)
    wkv_ref[own, :] = shard_ref[:, split:]
    weights_kv = Gather(torus, wkv_ref)
    weights_kv.start()

    count = tokens_ref.shape[0]

    def token_rows(step, part=None, flip=False):
        core = torus.place["core"]
        index = wrap(torus.place["z"] + step) * 2 + (1 - core if flip else core)
        size = count if part is None else count // 2
        start = index * count + (0 if part is None else part * (count // 2))
        return normed_ref.at[pl.ds(pl.multiple_of(start, count // 2), size), :]

    tokens = tokens_ref[...].astype(jnp.float32)
    token_rows(0)[...] = (tokens * inverse_rms(tokens) * norm_gain_ref[...]).astype(jnp.bfloat16)
    mine = token_rows(0)
    ring = {step: torus.send(mine, mine, "z", step) for step in (1, -1)}
    pair = {0: torus.send(mine, mine, "core", 1)}

    wq_ref[own, :] = shard_ref[:, :split]
    weights_q = Gather(torus, wq_ref)
    weights_kv.near()
    weights_q.start()
    onward = {}
    for step in (1, -1):
        torus.arrive(ring[step], token_rows(-step))
        piece = token_rows(-step, part_of(step))
        onward[step] = torus.send(piece, piece, "z", step)
        block = token_rows(-step)
        pair[-step] = torus.send(block, block, "core", 1)
    weights_kv.far()
    for step in (1, -1):
        torus.arrive(onward[step], token_rows(2, part_of(step)))
    block = token_rows(2)
    pair[2] = torus.send(block, block, "core", 1)
    weights_kv.cross((0, -1, 1))
    weights_q.near()
    weights_kv.cross((2,))
    weights_q.far()
    for step in (0, -1, 1, 2):
        torus.arrive(pair[step], token_rows(step, flip=True))
    weights_kv.finish()

    cosine, sine = cosine_ref[...], sine_ref[...]
    raw = jnp.dot(normed_ref[...], wkv_ref[...], preferred_element_type=jnp.float32)
    raw_ref[:, split:] = raw[:, :width]
    kv_ref[own, 0:width] = head_map(raw[:, :width], key_gain_ref[...], cosine, sine).astype(
        jnp.bfloat16
    )
    kv_ref[own, width:] = raw[:, width:].astype(jnp.bfloat16)
    keys_values = Gather(torus, kv_ref)
    keys_values.start()
    weights_q.cross((0, -1, 1))
    keys_values.near()
    weights_q.cross((2,))
    keys_values.far()
    weights_q.finish()
    keys_values.cross((0, -1, 1, 2))

    raw = jnp.dot(normed_ref[...], wq_ref[...], preferred_element_type=jnp.float32)
    raw_ref[:, :split] = raw
    for g in range(QUERY_PER_KEY):
        columns = slice(g * width, (g + 1) * width)
        q_ref[:, columns] = head_map(raw[:, columns], query_gain_ref[...], cosine, sine).astype(
            jnp.bfloat16
        )
    keys_values.finish()
    torus.close()


def project(tokens, shard, norm_gain, query_gain, key_gain, cosine, sine):
    rows, columns = shard.shape
    count, depth = tokens.shape
    local = cosine.shape[0]
    total = local * SIDE * SIDE
    width = HEAD_WIDTH
    split = QUERY_PER_KEY * width
    vmem = pl.BlockSpec(memory_space=pltpu.VMEM)
    copies = 3 * 40 + 8
    return pl.pallas_call(
        project_kernel,
        out_shape=(
            jax.ShapeDtypeStruct((local, split), jnp.bfloat16),
            jax.ShapeDtypeStruct((total, 2 * width), jnp.bfloat16),
            jax.ShapeDtypeStruct((local, split + width), jnp.float32),
            jax.ShapeDtypeStruct((local, depth), jnp.bfloat16),
            jax.ShapeDtypeStruct((depth, 2 * width), jnp.bfloat16),
            jax.ShapeDtypeStruct((depth, split), jnp.bfloat16),
        ),
        in_specs=[vmem] * 7,
        out_specs=(vmem,) * 6,
        scratch_shapes=[pltpu.SemaphoreType.DMA((copies,)), pltpu.SemaphoreType.DMA((copies,))],
        compiler_params=pltpu.CompilerParams(
            collective_id=0, has_side_effects=True, vmem_limit_bytes=48 * 1024 * 1024
        ),
        cost_estimate=pl.CostEstimate(
            flops=2 * local * depth * columns, bytes_accessed=2 * depth * columns, transcendentals=0
        ),
    )(tokens, shard, norm_gain, query_gain, key_gain, cosine, sine)


def attention_kernel(
    span_ref, q_ref, kv_ref, up_ref, bound_ref,
    context_ref, dq_ref, dkv_ref,
    exp_ref, q4_ref, up4_ref, num_ref, den_ref, dqt_ref,
):
    rows = q_ref.shape[0]
    width = HEAD_WIDTH
    block = KEY_BLOCK
    scale = width ** (-0.5)
    start_row = bound_ref[0:1, :]
    end_row = bound_ref[1:2, :]
    low, high = span_ref[0], span_ref[1]
    for g in range(QUERY_PER_KEY):
        q4_ref[g] = q_ref[:, g * width : (g + 1) * width]
    num_ref[...] = jnp.zeros_like(num_ref)
    den_ref[...] = jnp.zeros_like(den_ref)
    dqt_ref[...] = jnp.zeros_like(dqt_ref)
    dkv_ref[...] = jnp.zeros_like(dkv_ref)

    def forward(i, carry):
        at = pl.ds(pl.multiple_of(i * block, block), block)
        key = kv_ref[at, 0:width]
        value_t = kv_ref[at, width : 2 * width].T
        place = lax.broadcasted_iota(jnp.int32, (block, rows), 0) + i * block
        mask = (place >= start_row) & (place < end_row)
        for g in range(QUERY_PER_KEY):
            scores = lax.dot_general(
                key, q4_ref[g], NT, preferred_element_type=jnp.float32
            )
            exponent = jnp.where(mask, jnp.exp2(scores * (scale * LOG2E)), 0.0)
            den_ref[g] += jnp.sum(exponent.reshape(block // 8, 8, rows), axis=0)
            rounded = exponent.astype(jnp.bfloat16)
            exp_ref[g, at, :] = rounded
            num_ref[g] += jnp.dot(value_t, rounded, preferred_element_type=jnp.float32)
        return carry

    lax.fori_loop(low, high, forward, 0)
    corrections = []
    for g in range(QUERY_PER_KEY):
        columns = slice(g * width, (g + 1) * width)
        inverse = 1.0 / jnp.sum(den_ref[g], axis=0, keepdims=True)
        context_t = (num_ref[g] * inverse).astype(jnp.bfloat16).astype(jnp.float32)
        context_ref[:, columns] = context_t.T.astype(jnp.bfloat16)
        up_t = up_ref[:, columns].astype(jnp.float32).T
        up_t = (up_t * inverse).astype(jnp.bfloat16).astype(jnp.float32)
        up4_ref[g] = up_t.T.astype(jnp.bfloat16)
        corrections.append(jnp.sum(up_t * context_t, axis=0, keepdims=True))

    def backward(i, carry):
        at = pl.ds(pl.multiple_of(i * block, block), block)
        key_t = kv_ref[at, 0:width].T
        value = kv_ref[at, width : 2 * width]
        dk = jnp.zeros((block, width), jnp.float32)
        dv = jnp.zeros((block, width), jnp.float32)
        for g in range(QUERY_PER_KEY):
            grads = lax.dot_general(
                value, up4_ref[g], NT, preferred_element_type=jnp.float32
            )
            rounded = exp_ref[g, at, :]
            ds = (rounded.astype(jnp.float32) * (grads - corrections[g])).astype(jnp.bfloat16)
            dk += jnp.dot(ds, q4_ref[g], preferred_element_type=jnp.float32)
            dv += jnp.dot(rounded, up4_ref[g], preferred_element_type=jnp.float32)
            dqt_ref[g] += jnp.dot(key_t, ds, preferred_element_type=jnp.float32)
        dkv_ref[at, 0:width] = (dk * scale).astype(jnp.bfloat16)
        dkv_ref[at, width : 2 * width] = dv.astype(jnp.bfloat16)
        return carry

    lax.fori_loop(low, high, backward, 0)
    for g in range(QUERY_PER_KEY):
        dq_ref[:, g * width : (g + 1) * width] = (dqt_ref[g] * scale).T


def attention(span, queries, keys_values, upstream, bounds):
    rows = queries.shape[0]
    total = keys_values.shape[0]
    group = QUERY_PER_KEY
    vmem = pl.BlockSpec(memory_space=pltpu.VMEM)
    return pl.pallas_call(
        attention_kernel,
        out_shape=(
            jax.ShapeDtypeStruct((rows, group * HEAD_WIDTH), jnp.bfloat16),
            jax.ShapeDtypeStruct((rows, group * HEAD_WIDTH), jnp.float32),
            jax.ShapeDtypeStruct((total, 2 * HEAD_WIDTH), jnp.bfloat16),
        ),
        in_specs=[pl.BlockSpec(memory_space=pltpu.SMEM)] + [vmem] * 4,
        out_specs=(vmem, vmem, vmem),
        scratch_shapes=[
            pltpu.VMEM((group, total, rows), jnp.bfloat16),
            pltpu.VMEM((group, rows, HEAD_WIDTH), jnp.bfloat16),
            pltpu.VMEM((group, rows, HEAD_WIDTH), jnp.bfloat16),
            pltpu.VMEM((group, HEAD_WIDTH, rows), jnp.float32),
            pltpu.VMEM((group, 8, rows), jnp.float32),
            pltpu.VMEM((group, HEAD_WIDTH, rows), jnp.float32),
        ],
        compiler_params=pltpu.CompilerParams(vmem_limit_bytes=48 * 1024 * 1024),
        cost_estimate=pl.CostEstimate(
            flops=14 * group * rows * total * HEAD_WIDTH,
            bytes_accessed=8 * total * HEAD_WIDTH,
            transcendentals=group * rows * total,
        ),
    )(span, queries, keys_values, upstream, bounds)


def gradient_kernel(
    dq_ref, dkv_hbm, raw_ref, normed_hbm, wq_hbm, wkv_hbm, tokens_ref,
    norm_gain_ref, query_gain_ref, key_gain_ref, cosine_ref, sine_ref,
    token_grads_ref, projection_grads_ref, gains_ref,
    send_sems, recv_sems, local_sems,
    dkv_ref, normed_ref, wq_ref, wkv_ref, jq_ref, jkv_ref, gq_ref, gkv_ref, dkv_sum_ref,
    terms_ref, pair_ref, zfar_ref, znear_ref, gx_ref, gy_ref, gz_ref, gc_ref,
    *boxes,
):
    width = HEAD_WIDTH
    split = QUERY_PER_KEY * width
    torus = Torus(send_sems, recv_sems)
    loads = [
        pltpu.make_async_copy(source, target, local_sems.at[i])
        for i, (source, target) in enumerate(
            ((dkv_hbm, dkv_ref), (normed_hbm, normed_ref), (wq_hbm, wq_ref), (wkv_hbm, wkv_ref))
        )
    ]
    for load in loads:
        load.start()
    torus.greet((1, 2, 3))
    loads[0].wait()
    dkv = Scatter(torus, dkv_ref, *boxes[0:4])
    dwq = Scatter(torus, gq_ref, *boxes[4:8])
    dwkv = Scatter(torus, gkv_ref, *boxes[8:12])
    dkv.start()

    cosine, sine = cosine_ref[...], sine_ref[...]
    query_gain_grads = jnp.zeros((1, width), jnp.float32)
    for g in range(QUERY_PER_KEY):
        columns = slice(g * width, (g + 1) * width)
        raw_grads, gain_grads = head_map_back(
            raw_ref[:, columns], query_gain_ref[...], cosine, sine, dq_ref[:, columns]
        )
        jq_ref[:, columns] = raw_grads.astype(jnp.bfloat16)
        query_gain_grads = query_gain_grads + gain_grads
    loads[1].wait()

    def weight_grads(j_ref, g_ref):
        def body(i, carry):
            at = pl.ds(pl.multiple_of(i * 256, 256), 256)
            g_ref[at, :] = lax.dot_general(
                normed_ref[:, at], j_ref[...], TN, preferred_element_type=jnp.float32
            ).astype(jnp.bfloat16)
            return carry

        lax.fori_loop(0, normed_ref.shape[1] // 256, body, 0)

    weight_grads(jq_ref, gq_ref)
    dkv.turn()
    dwq.start()
    dkv.land()
    dkv.turn_two()
    dwq.turn((2, 1))

    def keep_dkv(at, total):
        dkv_sum_ref[at, :] = total

    dkv.finish(keep_dkv)
    raw_grads, key_gain_grads = head_map_back(
        raw_ref[:, split:], key_gain_ref[...], cosine, sine, dkv_sum_ref[:, :width]
    )
    jkv_ref[:, :width] = raw_grads.astype(jnp.bfloat16)
    jkv_ref[:, width:] = dkv_sum_ref[:, width:].astype(jnp.bfloat16)
    weight_grads(jkv_ref, gkv_ref)
    dwkv.start()
    dwq.turn((-1, 0))
    loads[2].wait()
    loads[3].wait()

    def input_terms(i, carry):
        at = pl.ds(pl.multiple_of(i * 256, 256), 256)
        terms_ref[:, at] = (
            lax.dot_general(jq_ref[...], wq_ref[at, :], NT, preferred_element_type=jnp.float32)
            + lax.dot_general(jkv_ref[...], wkv_ref[at, :], NT, preferred_element_type=jnp.float32)
        ).astype(jnp.bfloat16)
        return carry

    lax.fori_loop(0, terms_ref.shape[1] // 256, input_terms, 0)

    count = tokens_ref.shape[0]

    def term_rows(step, part=None, flip=False):
        core = torus.place["core"]
        index = wrap(torus.place["z"] + step) * 2 + (1 - core if flip else core)
        size = count if part is None else count // 2
        start = index * count + (0 if part is None else part * (count // 2))
        return terms_ref.at[pl.ds(pl.multiple_of(start, count // 2), size), :]

    pair = {
        step: torus.send(term_rows(step, flip=True), pair_ref.at[step % SIDE], "core", 1)
        for step in (2, 1, -1, 0)
    }
    dwq.land((2,))
    dwkv.turn((2,))
    far = {}
    torus.arrive(pair[2], pair_ref.at[2])
    add_to(term_rows(2), pair_ref.at[2])
    for step in (1, -1):
        far[step] = torus.send(
            term_rows(2, part_of(step)), zfar_ref.at[part_of(step)], "z", step
        )
    dwq.land((1, -1))
    dwq.turn_two()
    near = {}
    for step in (1, -1):
        torus.arrive(pair[step], pair_ref.at[step % SIDE])
        add_to(term_rows(step), pair_ref.at[step % SIDE])
        torus.arrive(far[step], zfar_ref.at[part_of(step)])
        add_to(term_rows(step, part_of(step)), zfar_ref.at[part_of(step)])
        near[step] = torus.send(term_rows(step), znear_ref.at[part_of(step)], "z", step)
    dwkv.turn((1, -1, 0))
    dwq.land((0,))
    torus.arrive(pair[0], pair_ref.at[0])
    for step in (1, -1):
        torus.arrive(near[step], znear_ref.at[part_of(step)])
    normed_grads = term_rows(0)[...].astype(jnp.float32) + pair_ref[0].astype(jnp.float32)
    normed_grads = normed_grads + (
        znear_ref[0].astype(jnp.float32) + znear_ref[1].astype(jnp.float32)
    )
    tokens = tokens_ref[...].astype(jnp.float32)
    inverse = inverse_rms(tokens)
    unit = tokens * inverse
    norm_gain_grads = jnp.sum(normed_grads * unit, axis=0, keepdims=True)
    scaled = normed_grads * norm_gain_ref[...]
    token_grads_ref[...] = inverse * (
        scaled - unit * jnp.mean(scaled * unit, axis=-1, keepdims=True)
    )
    lines, columns = gains_ref.shape
    run = tokens.shape[1] // lines
    gains_ref[...] = jnp.zeros_like(gains_ref)
    for i in range(lines):
        gains_ref[i : i + 1, 0:run] = norm_gain_grads[:, i * run : (i + 1) * run]
    gains_ref[0:1, run:] = query_gain_grads
    gains_ref[1:2, run:] = key_gain_grads

    def share(axis, box):
        place, size = torus.place[axis], box.shape[0]
        box[place] = gains_ref[...]
        return [
            torus.send(box.at[place], box.at[place], axis, step) for step in range(1, size)
        ]

    def collect(axis, box, sent):
        place, size = torus.place[axis], box.shape[0]
        for step in range(1, size):
            torus.arrive(sent[step - 1], box.at[lax.rem(place + size - step, size)])
        total = box[0]
        for i in range(1, size):
            total = total + box[i]
        gains_ref[...] = total

    def keep_q(at, total):
        projection_grads_ref[at, :split] = total

    def keep_kv(at, total):
        projection_grads_ref[at, split:] = total

    sent = share("z", gz_ref)
    dwkv.land((2, 1))
    collect("z", gz_ref, sent)
    sent = share("core", gc_ref)
    dwkv.land((-1,))
    collect("core", gc_ref, sent)
    sent = share("x", gx_ref)
    dwkv.turn_two()
    dwq.finish(keep_q)
    collect("x", gx_ref, sent)
    sent = share("y", gy_ref)
    dwkv.land((0,))
    dwkv.finish(keep_kv)
    collect("y", gy_ref, sent)
    torus.close()


def gradients(
    dq, dkv, raw, normed, wq, wkv, tokens, norm_gain, query_gain, key_gain, cosine, sine
):
    local, depth = normed.shape
    count = tokens.shape[0]
    total = dkv.shape[0]
    width = HEAD_WIDTH
    split = QUERY_PER_KEY * width
    rows = depth // (SIDE * SIDE)
    lines = 8
    gains = (lines, depth // lines + width)
    vmem = pl.BlockSpec(memory_space=pltpu.VMEM)
    anywhere = pl.BlockSpec(memory_space=pl.ANY)
    copies = 3 * 40 + 8 + 10
    bf16, f32 = jnp.bfloat16, jnp.float32
    return pl.pallas_call(
        gradient_kernel,
        out_shape=(
            jax.ShapeDtypeStruct((count, depth), f32),
            jax.ShapeDtypeStruct((rows, split + 2 * width), f32),
            jax.ShapeDtypeStruct(gains, f32),
        ),
        in_specs=[vmem, anywhere, vmem, anywhere, anywhere, anywhere] + [vmem] * 6,
        out_specs=(vmem,) * 3,
        scratch_shapes=[
            pltpu.SemaphoreType.DMA((copies,)),
            pltpu.SemaphoreType.DMA((copies,)),
            pltpu.SemaphoreType.DMA((4,)),
            pltpu.VMEM((total, 2 * width), bf16),
            pltpu.VMEM((local, depth), bf16),
            pltpu.VMEM((depth, split), bf16),
            pltpu.VMEM((depth, 2 * width), bf16),
            pltpu.VMEM((local, split), bf16),
            pltpu.VMEM((local, 2 * width), bf16),
            pltpu.VMEM((depth, split), bf16),
            pltpu.VMEM((depth, 2 * width), bf16),
            pltpu.VMEM((local, 2 * width), f32),
            pltpu.VMEM((local, depth), bf16),
            pltpu.VMEM((SIDE, count, depth), bf16),
            pltpu.VMEM((2, count // 2, depth), bf16),
            pltpu.VMEM((2, count, depth), bf16),
            pltpu.VMEM((SIDE,) + gains, f32),
            pltpu.VMEM((SIDE,) + gains, f32),
            pltpu.VMEM((SIDE,) + gains, f32),
            pltpu.VMEM((2,) + gains, f32),
        ]
        + scatter_scratch(total // (SIDE * SIDE), 2 * width)
        + scatter_scratch(rows, split)
        + scatter_scratch(rows, 2 * width),
        compiler_params=pltpu.CompilerParams(
            collective_id=1, has_side_effects=True, vmem_limit_bytes=56 * 1024 * 1024
        ),
        cost_estimate=pl.CostEstimate(
            flops=4 * local * depth * (split + 2 * width),
            bytes_accessed=4 * depth * (split + 2 * width),
            transcendentals=0,
        ),
    )(dq, dkv, raw, normed, wq, wkv, tokens, norm_gain, query_gain, key_gain, cosine, sine)


def rope_tables(positions, width):
    half = width // 2
    frequency = THETA ** (-2.0 * jnp.arange(half, dtype=jnp.float32) / width)
    angles = positions.astype(jnp.float32)[:, None] * frequency[None, :]
    cosine, sine = jnp.cos(angles), jnp.sin(angles)
    return (
        jnp.concatenate([cosine, cosine], axis=1),
        jnp.concatenate([-sine, sine], axis=1),
    )


def on_device(tokens, projection, norm_gain, query_gain, key_gain, segment_ids, context_cotangent):
    local = context_cotangent.shape[0]
    offset = lax.axis_index("ctx") * local
    positions = offset + jnp.arange(local, dtype=jnp.int32)
    cosine, sine = rope_tables(positions, HEAD_WIDTH)
    norm_gain = norm_gain.reshape(1, -1)
    query_gain = query_gain.reshape(1, -1)
    key_gain = key_gain.reshape(1, -1)
    query_segments = lax.dynamic_slice_in_dim(segment_ids, offset, local)
    starts = jnp.sum((segment_ids[:, None] < query_segments[None, :]).astype(jnp.int32), axis=0)
    ends = jnp.sum((segment_ids[:, None] <= query_segments[None, :]).astype(jnp.int32), axis=0)
    bounds = jnp.stack([starts, ends])
    span = jnp.stack([starts[0] // KEY_BLOCK, (ends[-1] + KEY_BLOCK - 1) // KEY_BLOCK])
    queries, keys_values, raw, normed, wkv, wq = project(
        tokens, projection, norm_gain, query_gain, key_gain, cosine, sine
    )
    context, query_grads, kv_grads = attention(
        span, queries, keys_values, context_cotangent, bounds
    )
    token_grads, projection_grads, gains = gradients(
        query_grads, kv_grads, raw, normed, wq, wkv, tokens,
        norm_gain, query_gain, key_gain, cosine, sine,
    )
    run = gains.shape[1] - HEAD_WIDTH
    return (
        context,
        token_grads,
        projection_grads,
        gains[:, :run].reshape(-1),
        gains[0, run:],
        gains[1, run:],
    )


def solution(mesh):
    placed = (
        P(("dp", "ctx", "tp"), None),
        P("ctx", "tp"),
        P(),
        P(),
        P(),
        P("dp"),
        P(("dp", "ctx"), "tp"),
    )
    return jax.shard_map(
        on_device,
        mesh=mesh,
        in_specs=placed,
        out_specs=(
            P(("dp", "ctx"), "tp"),
            P(("dp", "ctx", "tp"), None),
            P(("dp", "ctx"), "tp"),
            P("dp"),
            P("dp"),
            P("dp"),
        ),
        check_vma=False,
    )
```

time: 398 us -> 185 us (0.46)
  waiting for transfers between devices: 269 us -> 0 us
  Pallas kernels: 7.1 us -> 160 us
  blocking collectives: 68.5 us -> 0 us
  matrix products: 16.7 us -> 0 us
  between operations: 17.7 us -> 4 us
  local copies, waits for them, and re-layouts: 3.59 us -> 16.8 us
  other arithmetic: 13.6 us -> 3.25 us
    pallas_call x0 -> x2, Pallas kernels: none -> 154 us  [the longest x1 98.6 us: gradients(): pl.pallas_call(gradient_kernel, out_shape=(jax.ShapeDtypeStruct((count, d...]
    reduce_scatter x3 -> x0, waiting for transfers between devices: 139 us -> none  [the longest x1 98.2 us: on_device(): lax.psum_scatter(kv_grads, 'ctx', scatter_dimension=0, tiled=True)]
    all_gather x3 -> x0, waiting for transfers between devices: 129 us -> none  [the longest x1 63.3 us: on_device(): lax.all_gather(projection, 'ctx', axis=0, tiled=True)]
    psum x1 -> x0, blocking collectives: 68.5 us -> none  [on_device(): lax.psum((norm_gain_term, query_gain_term, key_gain_term), ('ctx', 'tp'))]
    dot_general x3 -> x0, matrix products: 16.7 us -> none  [the longest x1 6.18 us: on_device(): lax.dot_general(joined_gradient, lax.all_gather(projection, 'ctx', axis=0...]
    unnamed x18 -> x28, local copies, waits for them, and re-layouts: 1.83 us -> 13.7 us
  transfers between devices with their start and end apart: 6 -> 0, of which waited for: 6 -> 0; matrix products, arithmetic and copies ran while one was open for 3% -> 0% of each run, Pallas kernels for 0% -> 0%
where the time goes in v2:
time: 185 us; the launch traced here: 184 us
  Pallas kernels  160 us (86%)
  local copies, waits for them, and re-layouts  16.8 us (9%)
  between operations  4 us (2%)
  other arithmetic  3.25 us (2%)
    pallas_call x1, Pallas kernels, gradients(): pl.pallas_call(gradient_kernel, out_shape=(jax.ShapeDtypeStruct((count, d...  98.6 us
    pallas_call x1, Pallas kernels, project(): pl.pallas_call(project_kernel, out_shape=(jax.ShapeDtypeStruct((local, sp...  55.2 us
    unnamed x28, local copies, waits for them, and re-layouts  13.7 us
    pallas_call x1, Pallas kernels, attention(): pl.pallas_call(attention_kernel, out_shape=(jax.ShapeDtypeStruct((rows, g...  6.5 us

profile of v2, /device:TPU:1, one launch (start us, length us, event | category | flops | bytes accessed | tf_op | source)
XLA Modules:
  0.0 184.5 jit_solution(17245028413751924653)
XLA Ops:
  0.6 0.0 copy-start.11
  0.6 0.8 dynamic_slice.3
  1.5 2.5 %convert_reduce_fusion.1 = (s32[256]{0:T(256)S(1)}, s32[256]{0:T(256)S(1)}) fusion(s32[256]{0:T(256)S(1)} %dynamic_slice.3, s32[4096]{0:T(1024)} %param.12), kind=kLoop, calls=%fused_computation.1 | loop fusion | flops 6290944 | bytes 19456 | tf_op jit(solution)/shard_map/reduce_sum | solution.py:742
  3.9 0.6 slice.16
  5.2 0.5 slice.15
  8.3 0.1 pad_add_fusion.1.span_ref
  8.4 0.5 fusion
  9.0 0.1 pad_maximum_fusion
  9.1 0.0 copy-start.3
  9.1 0.0 copy-start.4
  9.1 0.0 copy-start.6
  9.1 1.0 copy-done.6
  10.2 0.0 copy-start.7
  10.2 0.7 copy-done.7
  10.9 0.0 copy-start.8
  10.9 0.7 copy-done.8
  11.5 0.0 copy-start.9
  11.5 0.7 copy-done.9
  12.2 0.0 copy-start.10
  12.2 1.0 copy-done.10
  13.2 55.2 %shard_map.118 = (bf16[256,512]{1,0:T(8,128)(2,1)S(1)}, bf16[4096,256]{1,0:T(8,128)(2,1)S(1)}, f32[256,640]{1,0:T(8,128)S(1)}, bf16[256,4096]{1,0:T(8,128)(2,1)S...) custom-call(bf16[32,4096]{1,0:T(8,128)(2,1)S(1)} %copy-done.6, bf16[256,768]{1,0:T(8,128)(2,1)S(1)} %copy-done.10, ...), custom_call_target="tpu_custom_call" | custom-call | flops 1610612736 | bytes 6291456 | tf_op jit(solution)/shard_map/pallas_call | solution.py:362
  68.4 0.0 copy-start
  68.4 1.4 copy-done
  69.8 0.0 copy-start.2
  69.8 0.8 copy-done.2
  70.6 0.0 copy-done.11
  70.6 6.5 %shard_map.119 = (bf16[256,512]{1,0:T(8,128)(2,1)}, f32[256,512]{1,0:T(8,128)S(1)}, bf16[4096,256]{1,0:T(8,128)(2,1)S(1)}) custom-call(s32[2]{0:T(128)S(1)} %pad_add_fusion.1.span_ref, bf16[256,512]{1,0:T(8,128)(2,1)S(1)} %get-tuple-element.18.q_ref, bf16[4096,256]{1,0:T(8,128)(2,1)S(1)} %get-tuple-element.19.kv_ref, bf16[256,512]{1,0:T(8,128)(2,1)S(1)} %copy-done.11, ...), custom_call_target="tpu_custom_call" | custom-call | flops 7516192768 | bytes 4194304 | tf_op jit(solution)/shard_map/pallas_call | solution.py:461
  77.1 0.0 copy-done.3
  77.1 0.0 copy-done.4
  77.1 0.0 copy-start.1
  77.1 1.3 copy-done.1
  78.5 0.0 copy-start.5
  78.5 0.8 copy-done.5
  79.3 98.6 %shard_map.120 = (f32[32,4096]{1,0:T(8,128)}, f32[256,768]{1,0:T(8,128)}, f32[8,640]{1,0:T(8,128)}) custom-call(f32[256,512]{1,0:T(8,128)} %copy-done.5, bf16[4096,256]{1,0:T(8,128)(2,1)} %copy-done.1, f32[256,640]{1,0:T(8,128)} %copy-done.2, bf16[256,4096]{1,0:T(8,128)(2,1)} %copy-done, bf16[4096,512]{1,0:T(8,128)(2,1)} %get-tuple-element.25.wq_hbm, ...), custom_call_target="tpu_custom_call" | custom-call | flops 3221225472 | bytes 12582912 | tf_op jit(solution)/shard_map/pallas_call | solution.py:677
  177.9 1.3 slice_bitcast_fusion.1
  179.2 0.7 slice_bitcast_fusion
  179.9 0.6 copy.13
  180.5 1.9 %copy.16 = f32[32,4096]{1,0:T(8,128)} copy(f32[32,4096]{1,0:T(8,128)} %get-tuple-element.46) | data formatting | bytes 1048576
  182.4 2.1 %copy.17 = f32[256,768]{1,0:T(8,128)} copy(f32[256,768]{1,0:T(8,128)} %get-tuple-element.47) | data formatting | bytes 1572864
  (3 shorter events, 0.0 us)
Async XLA Ops:
  0.6 70.0 %copy-start.11 = (bf16[256,512]{1,0:T(8,128)(2,1)S(1)}, bf16[256,512]{1,0:T(8,128)(2,1)}, u32[]{:S(2)}) copy-start(bf16[256,512]{1,0:T(8,128)(2,1)} %up_ref.1) | copy-start | bytes 786436
  9.1 68.0 %copy-start.3 = (f32[256,128]{1,0:T(8,128)}, f32[256,128]{1,0:T(8,128)S(1)}, u32[]{:S(2)}) copy-start(f32[256,128]{1,0:T(8,128)S(1)} %get-tuple-element.37.cosine_ref) | copy-start | bytes 393220
  9.1 68.0 %copy-start.4 = (f32[256,128]{1,0:T(8,128)}, f32[256,128]{1,0:T(8,128)S(1)}, u32[]{:S(2)}) copy-start(f32[256,128]{1,0:T(8,128)S(1)} %get-tuple-element.38.sine_ref) | copy-start | bytes 393220
  9.1 1.0 copy-start.6
  10.2 0.7 copy-start.7
  10.9 0.7 copy-start.8
  11.5 0.7 copy-start.9
  12.2 1.0 copy-start.10
  68.4 1.4 copy-start
  69.8 0.8 copy-start.2
  77.1 1.3 copy-start.1
  78.5 0.8 copy-start.5

commit v3 on v2

--- a/solution.py
+++ b/solution.py
@@ -1,5 +1,6 @@
 import jax
 import jax.numpy as jnp
+import numpy as np
 from jax import lax
 from jax.experimental import pallas as pl
 from jax.experimental.pallas import tpu as pltpu
@@ -7,7 +8,9 @@
 
 HEAD_WIDTH = 128
 QUERY_PER_KEY = 4
-KEY_BLOCK = 256
+KEY_BLOCK = 512
+ALIGN = 16
+SEGMENTS = 16
 SIDE = 4
 EPSILON = 1e-06
 THETA = 1000000.0
@@ -88,7 +91,7 @@
         self.rows = data.shape[0] // (SIDE * SIDE)
         self.keys = {}
 
-    def at(self, half, first, second, part=None):
+    def at(self, half, first, second, part=None, data=None):
         offset = dict(zip(self.orders[half], (first, second)))
         place = self.torus.place
         block = wrap(place["y"] + offset["y"]) * SIDE + wrap(place["x"] + offset["x"])
@@ -97,7 +100,8 @@
         if part is not None:
             start = start + part * (rows // 4)
         size = rows // 2 if part is None else rows // 4
-        return self.data.at[pl.ds(pl.multiple_of(start, rows // 4), size), :]
+        data = self.data if data is None else data
+        return data.at[pl.ds(pl.multiple_of(start, rows // 4), size), :]
 
     def send(self, key, source, target, axis, step):
         self.keys[key] = self.torus.send(source, target, axis, step)
@@ -167,13 +171,13 @@
         self.far_one, self.near_one = far_one, near_one
         self.far_two, self.near_two = far_two, near_two
 
-    def start(self, seconds=(2, 1, -1, 0)):
-        for second in seconds:
+    def start(self, data=None):
+        for second in (2, 1, -1, 0):
             for half in (0, 1):
                 for step in (1, -1):
                     self.send(
                         ("f1", half, second, step),
-                        self.at(half, 2, second, part_of(step)),
+                        self.at(half, 2, second, part_of(step), data),
                         self.far_one.at[half, second % SIDE, part_of(step)],
                         self.orders[half][0],
                         step,
@@ -269,18 +273,35 @@
 
 
 def project_kernel(
-    tokens_ref, shard_ref, norm_gain_ref, query_gain_ref, key_gain_ref, cosine_ref, sine_ref,
-    q_ref, kv_ref, raw_ref, normed_ref, wkv_ref, wq_ref,
-    send_sems, recv_sems,
+    tokens_hbm, shard_hbm, norm_gain_hbm, query_gain_hbm, key_gain_hbm, segments_hbm, waves_hbm,
+    q_ref, kv_ref, raw_ref, normed_ref, wkv_ref, wq_ref, rope_ref, bound_ref,
+    tokens_ref, norm_gain_ref, query_gain_ref, key_gain_ref, segments_ref, waves_ref,
+    send_sems, recv_sems, local_sems,
 ):
     width = HEAD_WIDTH
     split = QUERY_PER_KEY * width
     torus = Torus(send_sems, recv_sems)
-    torus.greet((1, -1))
-    rows = shard_ref.shape[0]
+    rows = shard_hbm.shape[0]
     ctx = lax.axis_index("ctx")
     own = pl.ds(pl.multiple_of(ctx * rows, rows), rows)
-    wkv_ref[own, :] = shard_ref[:, split:]
+    moves = (
+        (shard_hbm.at[:, split:], wkv_ref.at[own, :]),
+        (tokens_hbm, tokens_ref),
+        (norm_gain_hbm, norm_gain_ref),
+        (shard_hbm.at[:, 0:split], wq_ref.at[own, :]),
+        (waves_hbm, waves_ref),
+        (segments_hbm, segments_ref),
+        (query_gain_hbm, query_gain_ref),
+        (key_gain_hbm, key_gain_ref),
+    )
+    loads = [
+        pltpu.make_async_copy(source, target, local_sems.at[i])
+        for i, (source, target) in enumerate(moves)
+    ]
+    for load in loads:
+        load.start()
+    torus.greet((1, -1))
+    loads[0].wait()
     weights_kv = Gather(torus, wkv_ref)
     weights_kv.start()
 
@@ -293,16 +314,28 @@
         start = index * count + (0 if part is None else part * (count // 2))
         return normed_ref.at[pl.ds(pl.multiple_of(start, count // 2), size), :]
 
+    loads[1].wait()
+    loads[2].wait()
     tokens = tokens_ref[...].astype(jnp.float32)
     token_rows(0)[...] = (tokens * inverse_rms(tokens) * norm_gain_ref[...]).astype(jnp.bfloat16)
     mine = token_rows(0)
     ring = {step: torus.send(mine, mine, "z", step) for step in (1, -1)}
     pair = {0: torus.send(mine, mine, "core", 1)}
 
-    wq_ref[own, :] = shard_ref[:, :split]
+    loads[3].wait()
     weights_q = Gather(torus, wq_ref)
     weights_kv.near()
     weights_q.start()
+    for load in loads[4:]:
+        load.wait()
+    local = rope_ref.shape[1]
+    near_cosine, near_sine = waves_ref[0:local, :], waves_ref[local : 2 * local, :]
+
+    def far_wave(i):
+        return waves_ref[pl.ds(2 * local + i * SIDE * SIDE + ctx, 1), :]
+
+    rope_ref[0] = far_wave(0) * near_cosine - far_wave(1) * near_sine
+    rope_ref[1] = far_wave(3) * near_cosine + far_wave(2) * near_sine
     onward = {}
     for step in (1, -1):
         torus.arrive(ring[step], token_rows(-step))
@@ -318,200 +351,242 @@
     weights_kv.cross((0, -1, 1))
     weights_q.near()
     weights_kv.cross((2,))
+
+    segments = segments_ref[...]
+    lines = local // segments.shape[1]
+    for line in range(lines):
+        asked = segments_ref[pl.ds(ctx * lines + line, 1), :]
+        first = jnp.zeros(asked.shape, jnp.float32)
+        last = jnp.zeros(asked.shape, jnp.float32)
+        for number in range(SEGMENTS):
+            size = jnp.where(segments == number, 1.0, 0.0)
+            size = jnp.sum(jnp.sum(size, axis=0, keepdims=True), axis=1, keepdims=True)
+            first = first + jnp.where(asked > number, size, 0.0)
+            last = last + jnp.where(asked >= number, size, 0.0)
+        columns = slice(line * segments.shape[1], (line + 1) * segments.shape[1])
+        bound_ref[0:1, columns] = first
+        bound_ref[1:2, columns] = last
+
     weights_q.far()
     for step in (0, -1, 1, 2):
         torus.arrive(pair[step], token_rows(step, flip=True))
     weights_kv.finish()
 
-    cosine, sine = cosine_ref[...], sine_ref[...]
+    cosine, sine = rope_ref[0], rope_ref[1]
     raw = jnp.dot(normed_ref[...], wkv_ref[...], preferred_element_type=jnp.float32)
     raw_ref[:, split:] = raw[:, :width]
     kv_ref[own, 0:width] = head_map(raw[:, :width], key_gain_ref[...], cosine, sine).astype(
         jnp.bfloat16
     )
     kv_ref[own, width:] = raw[:, width:].astype(jnp.bfloat16)
+    weights_q.cross((0, -1, 1))
     keys_values = Gather(torus, kv_ref)
     keys_values.start()
-    weights_q.cross((0, -1, 1))
+    weights_q.cross((2,))
     keys_values.near()
-    weights_q.cross((2,))
+    weights_q.finish()
+
+    def query_head(g):
+        columns = slice(g * width, (g + 1) * width)
+        raw = jnp.dot(normed_ref[...], wq_ref[:, columns], preferred_element_type=jnp.float32)
+        raw_ref[:, columns] = raw
+        q_ref[:, columns] = head_map(raw, query_gain_ref[...], cosine, sine).astype(jnp.bfloat16)
+
     keys_values.far()
-    weights_q.finish()
-    keys_values.cross((0, -1, 1, 2))
-
-    raw = jnp.dot(normed_ref[...], wq_ref[...], preferred_element_type=jnp.float32)
-    raw_ref[:, :split] = raw
-    for g in range(QUERY_PER_KEY):
-        columns = slice(g * width, (g + 1) * width)
-        q_ref[:, columns] = head_map(raw[:, columns], query_gain_ref[...], cosine, sine).astype(
-            jnp.bfloat16
-        )
+    query_head(0)
+    keys_values.cross((0, -1))
+    query_head(1)
+    keys_values.cross((1, 2))
+    query_head(2)
+    query_head(3)
     keys_values.finish()
     torus.close()
 
 
-def project(tokens, shard, norm_gain, query_gain, key_gain, cosine, sine):
+def project(tokens, shard, norm_gain, query_gain, key_gain, segments, waves):
     rows, columns = shard.shape
     count, depth = tokens.shape
-    local = cosine.shape[0]
-    total = local * SIDE * SIDE
     width = HEAD_WIDTH
+    total = segments.shape[0] * segments.shape[1]
+    local = total // (SIDE * SIDE)
     split = QUERY_PER_KEY * width
     vmem = pl.BlockSpec(memory_space=pltpu.VMEM)
+    hbm = pl.BlockSpec(memory_space=pltpu.HBM)
     copies = 3 * 40 + 8
+    bf16, f32 = jnp.bfloat16, jnp.float32
     return pl.pallas_call(
         project_kernel,
         out_shape=(
-            jax.ShapeDtypeStruct((local, split), jnp.bfloat16),
-            jax.ShapeDtypeStruct((total, 2 * width), jnp.bfloat16),
-            jax.ShapeDtypeStruct((local, split + width), jnp.float32),
-            jax.ShapeDtypeStruct((local, depth), jnp.bfloat16),
-            jax.ShapeDtypeStruct((depth, 2 * width), jnp.bfloat16),
-            jax.ShapeDtypeStruct((depth, split), jnp.bfloat16),
-        ),
-        in_specs=[vmem] * 7,
-        out_specs=(vmem,) * 6,
-        scratch_shapes=[pltpu.SemaphoreType.DMA((copies,)), pltpu.SemaphoreType.DMA((copies,))],
+            jax.ShapeDtypeStruct((local, split), bf16),
+            jax.ShapeDtypeStruct((total, 2 * width), bf16),
+            jax.ShapeDtypeStruct((local, split + width), f32),
+            jax.ShapeDtypeStruct((local, depth), bf16),
+            jax.ShapeDtypeStruct((depth, 2 * width), bf16),
+            jax.ShapeDtypeStruct((depth, split), bf16),
+            jax.ShapeDtypeStruct((2, local, width), f32),
+            jax.ShapeDtypeStruct((2, local), f32),
+        ),
+        in_specs=[hbm] * 7,
+        out_specs=(vmem,) * 8,
+        scratch_shapes=[
+            pltpu.VMEM(tokens.shape, bf16),
+            pltpu.VMEM(norm_gain.shape, f32),
+            pltpu.VMEM(query_gain.shape, f32),
+            pltpu.VMEM(key_gain.shape, f32),
+            pltpu.VMEM(segments.shape, jnp.int32),
+            pltpu.VMEM(waves.shape, f32),
+            pltpu.SemaphoreType.DMA((copies,)),
+            pltpu.SemaphoreType.DMA((copies,)),
+            pltpu.SemaphoreType.DMA((8,)),
+        ],
         compiler_params=pltpu.CompilerParams(
-            collective_id=0, has_side_effects=True, vmem_limit_bytes=48 * 1024 * 1024
+            collective_id=0, has_side_effects=True, vmem_limit_bytes=24 * 1024 * 1024
         ),
         cost_estimate=pl.CostEstimate(
             flops=2 * local * depth * columns, bytes_accessed=2 * depth * columns, transcendentals=0
         ),
-    )(tokens, shard, norm_gain, query_gain, key_gain, cosine, sine)
+    )(tokens, shard, norm_gain, query_gain, key_gain, segments, waves)
 
 
 def attention_kernel(
-    span_ref, q_ref, kv_ref, up_ref, bound_ref,
+    q_ref, kv_ref, up_ref, bound_ref,
     context_ref, dq_ref, dkv_ref,
-    exp_ref, q4_ref, up4_ref, num_ref, den_ref, dqt_ref,
+    exp_ref, q4_ref, q4t_ref, up4_ref, up4t_ref, num_ref, den_ref, corr_ref,
 ):
     rows = q_ref.shape[0]
+    total = kv_ref.shape[0]
     width = HEAD_WIDTH
     block = KEY_BLOCK
     scale = width ** (-0.5)
     start_row = bound_ref[0:1, :]
     end_row = bound_ref[1:2, :]
-    low, high = span_ref[0], span_ref[1]
+    low = (jnp.min(start_row) * (1.0 / ALIGN)).astype(jnp.int32) * ALIGN
+    high = jnp.max(end_row).astype(jnp.int32)
+    steps = lax.div(high - low + (block - 1), block)
     for g in range(QUERY_PER_KEY):
-        q4_ref[g] = q_ref[:, g * width : (g + 1) * width]
+        query = q_ref[:, g * width : (g + 1) * width]
+        q4_ref[g] = query
+        q4t_ref[g] = query.T
     num_ref[...] = jnp.zeros_like(num_ref)
     den_ref[...] = jnp.zeros_like(den_ref)
-    dqt_ref[...] = jnp.zeros_like(dqt_ref)
+    dq_ref[...] = jnp.zeros_like(dq_ref)
     dkv_ref[...] = jnp.zeros_like(dkv_ref)
 
+    def rows_of(i):
+        wanted = low + i * block
+        first = jnp.minimum(wanted, total - block)
+        return wanted, first, pl.ds(pl.multiple_of(first, ALIGN), block)
+
     def forward(i, carry):
-        at = pl.ds(pl.multiple_of(i * block, block), block)
+        wanted, first, at = rows_of(i)
         key = kv_ref[at, 0:width]
-        value_t = kv_ref[at, width : 2 * width].T
-        place = lax.broadcasted_iota(jnp.int32, (block, rows), 0) + i * block
-        mask = (place >= start_row) & (place < end_row)
+        value = kv_ref[at, width : 2 * width]
+        place = (lax.broadcasted_iota(jnp.int32, (block, rows), 0) + first).astype(jnp.float32)
+        floor_row = jnp.maximum(start_row, wanted.astype(jnp.float32))
+        mask = (place >= floor_row) & (place < end_row)
         for g in range(QUERY_PER_KEY):
-            scores = lax.dot_general(
-                key, q4_ref[g], NT, preferred_element_type=jnp.float32
-            )
+            scores = jnp.dot(key, q4t_ref[g], preferred_element_type=jnp.float32)
             exponent = jnp.where(mask, jnp.exp2(scores * (scale * LOG2E)), 0.0)
             den_ref[g] += jnp.sum(exponent.reshape(block // 8, 8, rows), axis=0)
             rounded = exponent.astype(jnp.bfloat16)
-            exp_ref[g, at, :] = rounded
-            num_ref[g] += jnp.dot(value_t, rounded, preferred_element_type=jnp.float32)
+            exp_ref[g, pl.ds(pl.multiple_of(i * block, block), block), :] = rounded
+            num_ref[g] += lax.dot_general(
+                rounded, value, TN, preferred_element_type=jnp.float32
+            )
         return carry
 
-    lax.fori_loop(low, high, forward, 0)
-    corrections = []
+    lax.fori_loop(0, steps, forward, 0)
     for g in range(QUERY_PER_KEY):
         columns = slice(g * width, (g + 1) * width)
-        inverse = 1.0 / jnp.sum(den_ref[g], axis=0, keepdims=True)
-        context_t = (num_ref[g] * inverse).astype(jnp.bfloat16).astype(jnp.float32)
-        context_ref[:, columns] = context_t.T.astype(jnp.bfloat16)
-        up_t = up_ref[:, columns].astype(jnp.float32).T
-        up_t = (up_t * inverse).astype(jnp.bfloat16).astype(jnp.float32)
-        up4_ref[g] = up_t.T.astype(jnp.bfloat16)
-        corrections.append(jnp.sum(up_t * context_t, axis=0, keepdims=True))
+        inverse = 1.0 / jnp.sum(den_ref[g].T, axis=1, keepdims=True)
+        context = (num_ref[g] * inverse).astype(jnp.bfloat16)
+        context_ref[:, columns] = context
+        up = (up_ref[:, columns].astype(jnp.float32) * inverse).astype(jnp.bfloat16)
+        up4_ref[g] = up
+        up4t_ref[g] = up.T
+        product = up.astype(jnp.float32) * context.astype(jnp.float32)
+        corr_ref[g] = jnp.sum(product.T, axis=0, keepdims=True)
 
     def backward(i, carry):
-        at = pl.ds(pl.multiple_of(i * block, block), block)
-        key_t = kv_ref[at, 0:width].T
+        wanted, first, at = rows_of(i)
+        key = kv_ref[at, 0:width]
         value = kv_ref[at, width : 2 * width]
         dk = jnp.zeros((block, width), jnp.float32)
         dv = jnp.zeros((block, width), jnp.float32)
         for g in range(QUERY_PER_KEY):
-            grads = lax.dot_general(
-                value, up4_ref[g], NT, preferred_element_type=jnp.float32
-            )
-            rounded = exp_ref[g, at, :]
-            ds = (rounded.astype(jnp.float32) * (grads - corrections[g])).astype(jnp.bfloat16)
+            grads = jnp.dot(value, up4t_ref[g], preferred_element_type=jnp.float32)
+            rounded = exp_ref[g, pl.ds(pl.multiple_of(i * block, block), block), :]
+            ds = (rounded.astype(jnp.float32) * (grads - corr_ref[g])).astype(jnp.bfloat16)
             dk += jnp.dot(ds, q4_ref[g], preferred_element_type=jnp.float32)
             dv += jnp.dot(rounded, up4_ref[g], preferred_element_type=jnp.float32)
-            dqt_ref[g] += jnp.dot(key_t, ds, preferred_element_type=jnp.float32)
-        dkv_ref[at, 0:width] = (dk * scale).astype(jnp.bfloat16)
-        dkv_ref[at, width : 2 * width] = dv.astype(jnp.bfloat16)
+            dq_ref[:, g * width : (g + 1) * width] += lax.dot_general(
+                ds, key, TN, preferred_element_type=jnp.float32
+            )
+        kept = dkv_ref[at, :].astype(jnp.float32)
+        dkv_ref[at, 0:width] = (kept[:, 0:width] + dk * scale).astype(jnp.bfloat16)
+        dkv_ref[at, width : 2 * width] = (kept[:, width:] + dv).astype(jnp.bfloat16)
         return carry
 
-    lax.fori_loop(low, high, backward, 0)
-    for g in range(QUERY_PER_KEY):
-        dq_ref[:, g * width : (g + 1) * width] = (dqt_ref[g] * scale).T
-
-
-def attention(span, queries, keys_values, upstream, bounds):
+    lax.fori_loop(0, steps, backward, 0)
+    dq_ref[...] = dq_ref[...] * scale
+
+
+def attention(queries, keys_values, upstream, bounds):
     rows = queries.shape[0]
     total = keys_values.shape[0]
     group = QUERY_PER_KEY
+    width = HEAD_WIDTH
     vmem = pl.BlockSpec(memory_space=pltpu.VMEM)
+    bf16, f32 = jnp.bfloat16, jnp.float32
     return pl.pallas_call(
         attention_kernel,
         out_shape=(
-            jax.ShapeDtypeStruct((rows, group * HEAD_WIDTH), jnp.bfloat16),
-            jax.ShapeDtypeStruct((rows, group * HEAD_WIDTH), jnp.float32),
-            jax.ShapeDtypeStruct((total, 2 * HEAD_WIDTH), jnp.bfloat16),
-        ),
-        in_specs=[pl.BlockSpec(memory_space=pltpu.SMEM)] + [vmem] * 4,
+            jax.ShapeDtypeStruct((rows, group * width), bf16),
+            jax.ShapeDtypeStruct((rows, group * width), f32),
+            jax.ShapeDtypeStruct((total, 2 * width), bf16),
+        ),
+        in_specs=[vmem] * 4,
         out_specs=(vmem, vmem, vmem),
         scratch_shapes=[
-            pltpu.VMEM((group, total, rows), jnp.bfloat16),
-            pltpu.VMEM((group, rows, HEAD_WIDTH), jnp.bfloat16),
-            pltpu.VMEM((group, rows, HEAD_WIDTH), jnp.bfloat16),
-            pltpu.VMEM((group, HEAD_WIDTH, rows), jnp.float32),
-            pltpu.VMEM((group, 8, rows), jnp.float32),
-            pltpu.VMEM((group, HEAD_WIDTH, rows), jnp.float32),
+            pltpu.VMEM((group, total + KEY_BLOCK, rows), bf16),
+            pltpu.VMEM((group, rows, width), bf16),
+            pltpu.VMEM((group, width, rows), bf16),
+            pltpu.VMEM((group, rows, width), bf16),
+            pltpu.VMEM((group, width, rows), bf16),
+            pltpu.VMEM((group, rows, width), f32),
+            pltpu.VMEM((group, 8, rows), f32),
+            pltpu.VMEM((group, 1, rows), f32),
         ],
-        compiler_params=pltpu.CompilerParams(vmem_limit_bytes=48 * 1024 * 1024),
+        compiler_params=pltpu.CompilerParams(vmem_limit_bytes=28 * 1024 * 1024),
         cost_estimate=pl.CostEstimate(
-            flops=14 * group * rows * total * HEAD_WIDTH,
-            bytes_accessed=8 * total * HEAD_WIDTH,
+            flops=14 * group * rows * total * width,
+            bytes_accessed=8 * total * width,
             transcendentals=group * rows * total,
         ),
-    )(span, queries, keys_values, upstream, bounds)
+    )(queries, keys_values, upstream, bounds)
 
 
 def gradient_kernel(
-    dq_ref, dkv_hbm, raw_ref, normed_hbm, wq_hbm, wkv_hbm, tokens_ref,
-    norm_gain_ref, query_gain_ref, key_gain_ref, cosine_ref, sine_ref,
+    dq_ref, dkv_in_ref, raw_ref, normed_ref, wq_ref, wkv_ref, rope_ref, tokens_ref,
+    norm_gain_ref, query_gain_ref, key_gain_ref,
     token_grads_ref, projection_grads_ref, gains_ref,
     send_sems, recv_sems, local_sems,
-    dkv_ref, normed_ref, wq_ref, wkv_ref, jq_ref, jkv_ref, gq_ref, gkv_ref, dkv_sum_ref,
+    dkv_ref, jq_ref, jkv_ref, gq_ref, gkv_ref, dkv_sum_ref,
     terms_ref, pair_ref, zfar_ref, znear_ref, gx_ref, gy_ref, gz_ref, gc_ref,
     *boxes,
 ):
     width = HEAD_WIDTH
     split = QUERY_PER_KEY * width
     torus = Torus(send_sems, recv_sems)
-    loads = [
-        pltpu.make_async_copy(source, target, local_sems.at[i])
-        for i, (source, target) in enumerate(
-            ((dkv_hbm, dkv_ref), (normed_hbm, normed_ref), (wq_hbm, wq_ref), (wkv_hbm, wkv_ref))
-        )
-    ]
-    for load in loads:
-        load.start()
+    load = pltpu.make_async_copy(dkv_in_ref, dkv_ref, local_sems.at[0])
+    load.start()
     torus.greet((1, 2, 3))
-    loads[0].wait()
     dkv = Scatter(torus, dkv_ref, *boxes[0:4])
     dwq = Scatter(torus, gq_ref, *boxes[4:8])
     dwkv = Scatter(torus, gkv_ref, *boxes[8:12])
-    dkv.start()
-
-    cosine, sine = cosine_ref[...], sine_ref[...]
+    dkv.start(dkv_in_ref)
+
+    cosine, sine = rope_ref[0], rope_ref[1]
     query_gain_grads = jnp.zeros((1, width), jnp.float32)
     for g in range(QUERY_PER_KEY):
         columns = slice(g * width, (g + 1) * width)
@@ -520,7 +595,8 @@
         )
         jq_ref[:, columns] = raw_grads.astype(jnp.bfloat16)
         query_gain_grads = query_gain_grads + gain_grads
-    loads[1].wait()
+    load.wait()
+    dkv.turn()
 
     def weight_grads(j_ref, g_ref):
         def body(i, carry):
@@ -533,7 +609,6 @@
         lax.fori_loop(0, normed_ref.shape[1] // 256, body, 0)
 
     weight_grads(jq_ref, gq_ref)
-    dkv.turn()
     dwq.start()
     dkv.land()
     dkv.turn_two()
@@ -551,8 +626,6 @@
     weight_grads(jkv_ref, gkv_ref)
     dwkv.start()
     dwq.turn((-1, 0))
-    loads[2].wait()
-    loads[3].wait()
 
     def input_terms(i, carry):
         at = pl.ds(pl.multiple_of(i * 256, 256), 256)
@@ -612,13 +685,12 @@
     token_grads_ref[...] = inverse * (
         scaled - unit * jnp.mean(scaled * unit, axis=-1, keepdims=True)
     )
-    lines, columns = gains_ref.shape
-    run = tokens.shape[1] // lines
+    lines = tokens.shape[1] // width
     gains_ref[...] = jnp.zeros_like(gains_ref)
     for i in range(lines):
-        gains_ref[i : i + 1, 0:run] = norm_gain_grads[:, i * run : (i + 1) * run]
-    gains_ref[0:1, run:] = query_gain_grads
-    gains_ref[1:2, run:] = key_gain_grads
+        gains_ref[i : i + 1, :] = norm_gain_grads[:, i * width : (i + 1) * width]
+    gains_ref[lines : lines + 1, :] = query_gain_grads
+    gains_ref[lines + 1 : lines + 2, :] = key_gain_grads
 
     def share(axis, box):
         place, size = torus.place[axis], box.shape[0]
@@ -660,7 +732,7 @@
 
 
 def gradients(
-    dq, dkv, raw, normed, wq, wkv, tokens, norm_gain, query_gain, key_gain, cosine, sine
+    dq, dkv, raw, normed, wq, wkv, rope, tokens, norm_gain, query_gain, key_gain
 ):
     local, depth = normed.shape
     count = tokens.shape[0]
@@ -668,10 +740,8 @@
     width = HEAD_WIDTH
     split = QUERY_PER_KEY * width
     rows = depth // (SIDE * SIDE)
-    lines = 8
-    gains = (lines, depth // lines + width)
+    gains = (depth // width + 8, width)
     vmem = pl.BlockSpec(memory_space=pltpu.VMEM)
-    anywhere = pl.BlockSpec(memory_space=pl.ANY)
     copies = 3 * 40 + 8 + 10
     bf16, f32 = jnp.bfloat16, jnp.float32
     return pl.pallas_call(
@@ -681,16 +751,13 @@
             jax.ShapeDtypeStruct((rows, split + 2 * width), f32),
             jax.ShapeDtypeStruct(gains, f32),
         ),
-        in_specs=[vmem, anywhere, vmem, anywhere, anywhere, anywhere] + [vmem] * 6,
+        in_specs=[vmem] * 11,
         out_specs=(vmem,) * 3,
         scratch_shapes=[
             pltpu.SemaphoreType.DMA((copies,)),
             pltpu.SemaphoreType.DMA((copies,)),
-            pltpu.SemaphoreType.DMA((4,)),
+            pltpu.SemaphoreType.DMA((1,)),
             pltpu.VMEM((total, 2 * width), bf16),
-            pltpu.VMEM((local, depth), bf16),
-            pltpu.VMEM((depth, split), bf16),
-            pltpu.VMEM((depth, 2 * width), bf16),
             pltpu.VMEM((local, split), bf16),
             pltpu.VMEM((local, 2 * width), bf16),
             pltpu.VMEM((depth, split), bf16),
@@ -709,58 +776,92 @@
         + scatter_scratch(rows, split)
         + scatter_scratch(rows, 2 * width),
         compiler_params=pltpu.CompilerParams(
-            collective_id=1, has_side_effects=True, vmem_limit_bytes=56 * 1024 * 1024
+            collective_id=1, has_side_effects=True, vmem_limit_bytes=40 * 1024 * 1024
         ),
         cost_estimate=pl.CostEstimate(
             flops=4 * local * depth * (split + 2 * width),
             bytes_accessed=4 * depth * (split + 2 * width),
             transcendentals=0,
         ),
-    )(dq, dkv, raw, normed, wq, wkv, tokens, norm_gain, query_gain, key_gain, cosine, sine)
-
-
-def rope_tables(positions, width):
+    )(dq, dkv, raw, normed, wq, wkv, rope, tokens, norm_gain, query_gain, key_gain)
+
+
+def finish_kernel(
+    token_ref, projection_ref, gains_ref,
+    token_out, projection_out, norm_out, query_out, key_out,
+    sems,
+):
+    copies = [
+        pltpu.make_async_copy(token_ref, token_out, sems.at[0]),
+        pltpu.make_async_copy(projection_ref, projection_out, sems.at[1]),
+    ]
+    for copy in copies:
+        copy.start()
+    lines = norm_out.shape[0]
+    norm_out[...] = gains_ref[0:lines, :]
+    query_out[...] = gains_ref[lines : lines + 1, :]
+    key_out[...] = gains_ref[lines + 1 : lines + 2, :]
+    for copy in copies:
+        copy.wait()
+
+
+def finish(token_grads, projection_grads, gains):
+    width = HEAD_WIDTH
+    vmem = pl.BlockSpec(memory_space=pltpu.VMEM)
+    hbm = pl.BlockSpec(memory_space=pltpu.HBM)
+    anywhere = pl.BlockSpec(memory_space=pl.ANY)
+    f32 = jnp.float32
+    return pl.pallas_call(
+        finish_kernel,
+        out_shape=(
+            jax.ShapeDtypeStruct(token_grads.shape, f32),
+            jax.ShapeDtypeStruct(projection_grads.shape, f32),
+            jax.ShapeDtypeStruct((token_grads.shape[1] // width, width), f32),
+            jax.ShapeDtypeStruct((1, width), f32),
+            jax.ShapeDtypeStruct((1, width), f32),
+        ),
+        in_specs=[anywhere, anywhere, vmem],
+        out_specs=(hbm, hbm, vmem, vmem, vmem),
+        scratch_shapes=[pltpu.SemaphoreType.DMA((2,))],
+        compiler_params=pltpu.CompilerParams(vmem_limit_bytes=4 * 1024 * 1024),
+    )(token_grads, projection_grads, gains)
+
+
+def rope_waves(local, blocks, width):
     half = width // 2
-    frequency = THETA ** (-2.0 * jnp.arange(half, dtype=jnp.float32) / width)
-    angles = positions.astype(jnp.float32)[:, None] * frequency[None, :]
-    cosine, sine = jnp.cos(angles), jnp.sin(angles)
-    return (
-        jnp.concatenate([cosine, cosine], axis=1),
-        jnp.concatenate([-sine, sine], axis=1),
-    )
+    frequency = THETA ** (-2.0 * np.arange(half) / width)
+    frequency = np.concatenate([frequency, frequency])
+    sign = np.concatenate([-np.ones(half), np.ones(half)])
+    near = np.arange(local)[:, None] * frequency[None, :]
+    far = np.arange(blocks)[:, None] * float(local) * frequency[None, :]
+    waves = [np.cos(near), np.sin(near), np.cos(far), np.sin(far), sign * np.cos(far), sign * np.sin(far)]
+    return np.concatenate(waves, axis=0).astype(np.float32)
 
 
 def on_device(tokens, projection, norm_gain, query_gain, key_gain, segment_ids, context_cotangent):
     local = context_cotangent.shape[0]
-    offset = lax.axis_index("ctx") * local
-    positions = offset + jnp.arange(local, dtype=jnp.int32)
-    cosine, sine = rope_tables(positions, HEAD_WIDTH)
+    waves = jnp.asarray(rope_waves(local, SIDE * SIDE, HEAD_WIDTH))
     norm_gain = norm_gain.reshape(1, -1)
     query_gain = query_gain.reshape(1, -1)
     key_gain = key_gain.reshape(1, -1)
-    query_segments = lax.dynamic_slice_in_dim(segment_ids, offset, local)
-    starts = jnp.sum((segment_ids[:, None] < query_segments[None, :]).astype(jnp.int32), axis=0)
-    ends = jnp.sum((segment_ids[:, None] <= query_segments[None, :]).astype(jnp.int32), axis=0)
-    bounds = jnp.stack([starts, ends])
-    span = jnp.stack([starts[0] // KEY_BLOCK, (ends[-1] + KEY_BLOCK - 1) // KEY_BLOCK])
-    queries, keys_values, raw, normed, wkv, wq = project(
-        tokens, projection, norm_gain, query_gain, key_gain, cosine, sine
-    )
-    context, query_grads, kv_grads = attention(
-        span, queries, keys_values, context_cotangent, bounds
-    )
+    segments = segment_ids.reshape(-1, 128)
+    queries, keys_values, raw, normed, wkv, wq, rope, bounds = project(
+        tokens, projection, norm_gain, query_gain, key_gain, segments, waves
+    )
+    context, query_grads, kv_grads = attention(queries, keys_values, context_cotangent, bounds)
     token_grads, projection_grads, gains = gradients(
-        query_grads, kv_grads, raw, normed, wq, wkv, tokens,
-        norm_gain, query_gain, key_gain, cosine, sine,
-    )
-    run = gains.shape[1] - HEAD_WIDTH
+        query_grads, kv_grads, raw, normed, wq, wkv, rope, tokens, norm_gain, query_gain, key_gain
+    )
+    token_grads, projection_grads, norm_gains, query_gains, key_gains = finish(
+        token_grads, projection_grads, gains
+    )
     return (
         context,
         token_grads,
         projection_grads,
-        gains[:, :run].reshape(-1),
-        gains[0, run:],
-        gains[1, run:],
+        norm_gains.reshape(-1),
+        query_gains.reshape(-1),
+        key_gains.reshape(-1),
     )
 
 

time: 185 us -> 148 us (0.80)
  Pallas kernels: 160 us -> 142 us
  local copies, waits for them, and re-layouts: 16.8 us -> 5.67 us
  other arithmetic: 3.25 us -> 0 us
  between operations: 4 us -> 0.87 us
    pallas_call x1, Pallas kernels: 98.6 us -> 68.6 us  [gradients(): pl.pallas_call(gradient_kernel, out_shape=(jax.ShapeDtypeStruct((count, d...]
    pallas_call x1, Pallas kernels: 6.5 us -> 19.2 us  [attention(): pl.pallas_call(attention_kernel, out_shape=(jax.ShapeDtypeStruct((rows, g...]
    unnamed x28 -> x24, local copies, waits for them, and re-layouts: 13.7 us -> 5.67 us
    pallas_call x1, Pallas kernels: 55.2 us -> 52.1 us  [project(): pl.pallas_call(project_kernel, out_shape=(jax.ShapeDtypeStruct((local, sp...]
    reduce_sum x1 -> x0, other arithmetic: 2.48 us -> none  [on_device(): jnp.sum((segment_ids[:, None] < query_segments[None, :]).astype(jnp.int32...]
where the time goes in v3:
time: 148 us
  Pallas kernels  142 us (96%)
  local copies, waits for them, and re-layouts  5.67 us (4%)
    pallas_call x1, Pallas kernels, gradients(): pl.pallas_call(gradient_kernel, out_shape=(jax.ShapeDtypeStruct((count, d...  68.6 us
    pallas_call x1, Pallas kernels, project(): pl.pallas_call(project_kernel, out_shape=(jax.ShapeDtypeStruct((local, sp...  52.1 us
    pallas_call x1, Pallas kernels, attention(): pl.pallas_call(attention_kernel, out_shape=(jax.ShapeDtypeStruct((rows, g...  19.2 us
    unnamed x24, local copies, waits for them, and re-layouts  5.67 us

profile of v3, /device:TPU:1, one launch (start us, length us, event | category | flops | bytes accessed | tf_op | source)
XLA Modules:
  0.0 148.1 jit_solution(13063609753897399304)
XLA Ops:
  0.6 0.0 copy-start
  0.6 0.9 copy-done
  1.6 0.0 copy-start.2
  1.6 0.7 copy-done.2
  2.3 0.0 copy-start.4
  2.3 0.7 copy-done.4
  3.0 0.0 copy-start.6
  3.0 0.7 copy-done.6
  3.6 0.0 copy-start.8
  3.6 1.0 copy-done.8
  4.6 0.0 copy-start.10
  4.6 0.7 copy-done.10
  5.3 0.0 copy-start.11
  5.3 1.0 copy-done.11
  6.3 0.0 copy-start.9
  6.3 52.1 %shard_map.127 = (bf16[256,512]{1,0:T(8,128)(2,1)S(1)}, bf16[4096,256]{1,0:T(8,128)(2,1)S(1)}, f32[256,640]{1,0:T(8,128)S(1)}, bf16[256,4096]{1,0:T(8,128)(2,1)S...) custom-call(bf16[32,4096]{1,0:T(8,128)(2,1)S(1)} %copy-done, ...), custom_call_target="tpu_custom_call" | custom-call | flops 1610612736 | bytes 6291456 | tf_op jit(solution)/shard_map/pallas_call | solution.py:417
  58.4 0.0 copy-done.9
  58.4 0.0 copy-start.1
  58.4 0.0 copy-start.3
  58.4 0.0 copy-start.5
  58.4 0.0 copy-start.7
  58.4 19.2 %shard_map.128 = (bf16[256,512]{1,0:T(8,128)(2,1)}, f32[256,512]{1,0:T(8,128)S(1)}, bf16[4096,256]{1,0:T(8,128)(2,1)S(1)}) custom-call(bf16[256,512]{1,0:T(8,128)(2,1)S(1)} %get-tuple-element.25.q_ref, bf16[4096,256]{1,0:T(8,128)(2,1)S(1)} %get-tuple-element.26.kv_ref, bf16[256,512]{1,0:T(8,128)(2,1)S(1)} %copy-done.9, f32[2,256]{1,0:T(2,128)S(1)} %get-tuple-element.27.bound_ref), custom_call_target="tpu_custom_call" | custom-call | flops 7516192768 | bytes 4194304 | tf_op jit(solution)/shard_map/pallas_call | solution.py:541
  77.6 0.0 copy-done.1
  77.6 0.0 copy-done.3
  77.6 0.0 copy-done.5
  77.6 0.0 copy-done.7
  77.6 68.6 %shard_map.129 = (f32[32,4096]{1,0:T(8,128)S(1)}, f32[256,768]{1,0:T(8,128)S(1)}, f32[40,128]{1,0:T(8,128)S(1)}) custom-call(f32[256,512]{1,0:T(8,128)S(1)} %get-tuple-element.29.dq_ref, bf16[4096,256]{1,0:T(8,128)(2,1)S(1)} %get-tuple-element.30.dkv_in_ref, f32[256,640]{1,0:T(8,128)S(1)} %get-tuple-element.31.raw_ref, ...), custom_call_target="tpu_custom_call" | custom-call | flops 3221225472 | bytes 12582912 | tf_op jit(solution)/shard_map/pallas_call | solution.py:747
  146.2 1.7 %shard_map.130 = (f32[32,4096]{1,0:T(8,128)}, f32[256,768]{1,0:T(8,128)}, f32[32,128]{1,0:T(8,128)}, f32[1,128]{1,0:T(1,128)}, f32[1,128]{1,0:T(1,128)}) custom-call(f32[32,4096]{1,0:T(8,128)S(1)} %get-tuple-element.36.token_ref, f32[256,768]{1,0:T(8,128)S(1)} %get-tuple-element.37.projection_ref, f32[40,128]{1,0:T(8,128)S(1)} %get-tuple-element.38.gains_ref), custom_call_target="tpu_custom_call" | custom-call | tf_op jit(solution)/shard_map/pallas_call | solution.py:814
Async XLA Ops:
  0.6 1.0 copy-start
  1.6 0.7 copy-start.2
  2.3 0.7 copy-start.4
  3.0 0.7 copy-start.6
  3.6 1.0 copy-start.8
  4.6 0.7 copy-start.10
  5.3 1.0 copy-start.11
  6.3 52.1 %copy-start.9 = (bf16[256,512]{1,0:T(8,128)(2,1)S(1)}, bf16[256,512]{1,0:T(8,128)(2,1)}, u32[]{:S(2)}) copy-start(bf16[256,512]{1,0:T(8,128)(2,1)} %up_ref.1) | copy-start | bytes 786436
  58.4 19.2 %copy-start.1 = (bf16[32,4096]{1,0:T(8,128)(2,1)S(1)}, bf16[32,4096]{1,0:T(8,128)(2,1)}, u32[]{:S(2)}) copy-start(bf16[32,4096]{1,0:T(8,128)(2,1)} %tokens_ref.1) | copy-start | bytes 786436
  58.4 19.2 %copy-start.3 = (f32[4096]{0:T(1024)S(1)}, f32[4096]{0:T(1024)}, u32[]{:S(2)}) copy-start(f32[4096]{0:T(1024)} %param.10) | copy-start | bytes 49156
  58.4 19.2 %copy-start.5 = (f32[128]{0:T(128)S(1)}, f32[128]{0:T(128)}, u32[]{:S(2)}) copy-start(f32[128]{0:T(128)} %param.11) | copy-start | bytes 1540
  58.4 19.2 %copy-start.7 = (f32[128]{0:T(128)S(1)}, f32[128]{0:T(128)}, u32[]{:S(2)}) copy-start(f32[128]{0:T(128)} %param.12) | copy-start | bytes 1540

commit v4 on v3

--- a/solution.py
+++ b/solution.py
@@ -8,8 +8,6 @@
 
 HEAD_WIDTH = 128
 QUERY_PER_KEY = 4
-KEY_BLOCK = 512
-ALIGN = 16
 SEGMENTS = 16
 SIDE = 4
 EPSILON = 1e-06
@@ -91,7 +89,7 @@
         self.rows = data.shape[0] // (SIDE * SIDE)
         self.keys = {}
 
-    def at(self, half, first, second, part=None, data=None):
+    def at(self, half, first, second, part=None):
         offset = dict(zip(self.orders[half], (first, second)))
         place = self.torus.place
         block = wrap(place["y"] + offset["y"]) * SIDE + wrap(place["x"] + offset["x"])
@@ -100,8 +98,7 @@
         if part is not None:
             start = start + part * (rows // 4)
         size = rows // 2 if part is None else rows // 4
-        data = self.data if data is None else data
-        return data.at[pl.ds(pl.multiple_of(start, rows // 4), size), :]
+        return self.data.at[pl.ds(pl.multiple_of(start, rows // 4), size), :]
 
     def send(self, key, source, target, axis, step):
         self.keys[key] = self.torus.send(source, target, axis, step)
@@ -171,22 +168,22 @@
         self.far_one, self.near_one = far_one, near_one
         self.far_two, self.near_two = far_two, near_two
 
-    def start(self, data=None):
+    def start(self, halves=(0, 1)):
         for second in (2, 1, -1, 0):
-            for half in (0, 1):
+            for half in halves:
                 for step in (1, -1):
                     self.send(
                         ("f1", half, second, step),
-                        self.at(half, 2, second, part_of(step), data),
+                        self.at(half, 2, second, part_of(step)),
                         self.far_one.at[half, second % SIDE, part_of(step)],
                         self.orders[half][0],
                         step,
                     )
 
-    def turn(self, seconds=(2, 1, -1, 0)):
+    def turn(self, seconds=(2, 1, -1, 0), steps=(1, -1)):
         for second in seconds:
             for half in (0, 1):
-                for step in (1, -1):
+                for step in steps:
                     landed = self.far_one.at[half, second % SIDE, part_of(step)]
                     self.arrive(("f1", half, second, step), landed)
                     add_to(self.at(half, step, second, part_of(step)), landed)
@@ -272,27 +269,35 @@
     return raw_grads, gain_grads
 
 
-def project_kernel(
-    tokens_hbm, shard_hbm, norm_gain_hbm, query_gain_hbm, key_gain_hbm, segments_hbm, waves_hbm,
-    q_ref, kv_ref, raw_ref, normed_ref, wkv_ref, wq_ref, rope_ref, bound_ref,
-    tokens_ref, norm_gain_ref, query_gain_ref, key_gain_ref, segments_ref, waves_ref,
+def layer_kernel(
+    tokens_hbm, shard_hbm, norm_gain_hbm, query_gain_hbm, key_gain_hbm, segments_hbm, waves_hbm, up_hbm,
+    context_ref, token_grads_ref, projection_grads_ref, gains_ref,
     send_sems, recv_sems, local_sems,
+    tokens_ref, norm_gain_ref, query_gain_ref, key_gain_ref, segments_ref, waves_ref, up_ref,
+    kv_ref, raw_ref, normed_ref, wkv_ref, wqa_ref, wqb_ref, rope_ref, bound_ref,
+    exp_ref, q4_ref, q4t_ref, up4_ref, up4t_ref, num_ref, den_ref, corr_ref, dq_ref,
+    dkv_ref, jq_ref, jkv_ref, gq_ref, gkv_ref, dkv_sum_ref,
+    terms_ref, pair_ref, zfar_ref, znear_ref, gx_ref, gy_ref, gz_ref, gc_ref,
+    *boxes,
 ):
     width = HEAD_WIDTH
     split = QUERY_PER_KEY * width
+    pair_width = 2 * width
     torus = Torus(send_sems, recv_sems)
     rows = shard_hbm.shape[0]
     ctx = lax.axis_index("ctx")
     own = pl.ds(pl.multiple_of(ctx * rows, rows), rows)
     moves = (
-        (shard_hbm.at[:, split:], wkv_ref.at[own, :]),
+        (shard_hbm.at[:, 0:pair_width], wqa_ref.at[own, :]),
         (tokens_hbm, tokens_ref),
         (norm_gain_hbm, norm_gain_ref),
-        (shard_hbm.at[:, 0:split], wq_ref.at[own, :]),
+        (shard_hbm.at[:, split:], wkv_ref.at[own, :]),
+        (shard_hbm.at[:, pair_width:split], wqb_ref.at[own, :]),
         (waves_hbm, waves_ref),
         (segments_hbm, segments_ref),
         (query_gain_hbm, query_gain_ref),
         (key_gain_hbm, key_gain_ref),
+        (up_hbm, up_ref),
     )
     loads = [
         pltpu.make_async_copy(source, target, local_sems.at[i])
@@ -300,10 +305,13 @@
     ]
     for load in loads:
         load.start()
-    torus.greet((1, -1))
+    torus.greet((1, 2, 3))
     loads[0].wait()
+    weights_qa = Gather(torus, wqa_ref)
     weights_kv = Gather(torus, wkv_ref)
-    weights_kv.start()
+    weights_qb = Gather(torus, wqb_ref)
+    keys_values = Gather(torus, kv_ref)
+    weights_qa.start()
 
     count = tokens_ref.shape[0]
 
@@ -323,9 +331,8 @@
     pair = {0: torus.send(mine, mine, "core", 1)}
 
     loads[3].wait()
-    weights_q = Gather(torus, wq_ref)
-    weights_kv.near()
-    weights_q.start()
+    weights_qa.near()
+    weights_kv.start()
     for load in loads[4:]:
         load.wait()
     local = rope_ref.shape[1]
@@ -343,14 +350,15 @@
         onward[step] = torus.send(piece, piece, "z", step)
         block = token_rows(-step)
         pair[-step] = torus.send(block, block, "core", 1)
-    weights_kv.far()
+    weights_qa.far()
     for step in (1, -1):
         torus.arrive(onward[step], token_rows(2, part_of(step)))
     block = token_rows(2)
     pair[2] = torus.send(block, block, "core", 1)
-    weights_kv.cross((0, -1, 1))
-    weights_q.near()
-    weights_kv.cross((2,))
+    weights_qa.cross((0, -1, 1))
+    weights_kv.near()
+    weights_qa.cross((2,))
+    weights_qb.start()
 
     segments = segments_ref[...]
     lines = local // segments.shape[1]
@@ -367,135 +375,114 @@
         bound_ref[0:1, columns] = first
         bound_ref[1:2, columns] = last
 
-    weights_q.far()
+    weights_kv.far()
     for step in (0, -1, 1, 2):
         torus.arrive(pair[step], token_rows(step, flip=True))
+    weights_qa.finish()
+    cosine, sine = rope_ref[0], rope_ref[1]
+
+    def query_heads(weights_ref, heads):
+        both = jnp.dot(normed_ref[...], weights_ref[...], preferred_element_type=jnp.float32)
+        for i, g in enumerate(heads):
+            raw = both[:, i * width : (i + 1) * width]
+            raw_ref[:, g * width : (g + 1) * width] = raw
+            query = head_map(raw, query_gain_ref[...], cosine, sine).astype(jnp.bfloat16)
+            q4_ref[g] = query
+            q4t_ref[g] = query.T
+
+    weights_kv.cross((0, -1))
+    query_heads(wqa_ref, (0, 1))
+    weights_kv.cross((1,))
+    weights_qb.near()
+    weights_kv.cross((2,))
+    weights_qb.far()
     weights_kv.finish()
-
-    cosine, sine = rope_ref[0], rope_ref[1]
     raw = jnp.dot(normed_ref[...], wkv_ref[...], preferred_element_type=jnp.float32)
     raw_ref[:, split:] = raw[:, :width]
     kv_ref[own, 0:width] = head_map(raw[:, :width], key_gain_ref[...], cosine, sine).astype(
         jnp.bfloat16
     )
     kv_ref[own, width:] = raw[:, width:].astype(jnp.bfloat16)
-    weights_q.cross((0, -1, 1))
-    keys_values = Gather(torus, kv_ref)
+    weights_qb.cross((0, -1, 1))
     keys_values.start()
-    weights_q.cross((2,))
+    weights_qb.cross((2,))
     keys_values.near()
-    weights_q.finish()
-
-    def query_head(g):
-        columns = slice(g * width, (g + 1) * width)
-        raw = jnp.dot(normed_ref[...], wq_ref[:, columns], preferred_element_type=jnp.float32)
-        raw_ref[:, columns] = raw
-        q_ref[:, columns] = head_map(raw, query_gain_ref[...], cosine, sine).astype(jnp.bfloat16)
-
-    keys_values.far()
-    query_head(0)
-    keys_values.cross((0, -1))
-    query_head(1)
-    keys_values.cross((1, 2))
-    query_head(2)
-    query_head(3)
-    keys_values.finish()
-    torus.close()
-
-
-def project(tokens, shard, norm_gain, query_gain, key_gain, segments, waves):
-    rows, columns = shard.shape
-    count, depth = tokens.shape
-    width = HEAD_WIDTH
-    total = segments.shape[0] * segments.shape[1]
-    local = total // (SIDE * SIDE)
-    split = QUERY_PER_KEY * width
-    vmem = pl.BlockSpec(memory_space=pltpu.VMEM)
-    hbm = pl.BlockSpec(memory_space=pltpu.HBM)
-    copies = 3 * 40 + 8
-    bf16, f32 = jnp.bfloat16, jnp.float32
-    return pl.pallas_call(
-        project_kernel,
-        out_shape=(
-            jax.ShapeDtypeStruct((local, split), bf16),
-            jax.ShapeDtypeStruct((total, 2 * width), bf16),
-            jax.ShapeDtypeStruct((local, split + width), f32),
-            jax.ShapeDtypeStruct((local, depth), bf16),
-            jax.ShapeDtypeStruct((depth, 2 * width), bf16),
-            jax.ShapeDtypeStruct((depth, split), bf16),
-            jax.ShapeDtypeStruct((2, local, width), f32),
-            jax.ShapeDtypeStruct((2, local), f32),
-        ),
-        in_specs=[hbm] * 7,
-        out_specs=(vmem,) * 8,
-        scratch_shapes=[
-            pltpu.VMEM(tokens.shape, bf16),
-            pltpu.VMEM(norm_gain.shape, f32),
-            pltpu.VMEM(query_gain.shape, f32),
-            pltpu.VMEM(key_gain.shape, f32),
-            pltpu.VMEM(segments.shape, jnp.int32),
-            pltpu.VMEM(waves.shape, f32),
-            pltpu.SemaphoreType.DMA((copies,)),
-            pltpu.SemaphoreType.DMA((copies,)),
-            pltpu.SemaphoreType.DMA((8,)),
-        ],
-        compiler_params=pltpu.CompilerParams(
-            collective_id=0, has_side_effects=True, vmem_limit_bytes=24 * 1024 * 1024
-        ),
-        cost_estimate=pl.CostEstimate(
-            flops=2 * local * depth * columns, bytes_accessed=2 * depth * columns, transcendentals=0
-        ),
-    )(tokens, shard, norm_gain, query_gain, key_gain, segments, waves)
-
-
-def attention_kernel(
-    q_ref, kv_ref, up_ref, bound_ref,
-    context_ref, dq_ref, dkv_ref,
-    exp_ref, q4_ref, q4t_ref, up4_ref, up4t_ref, num_ref, den_ref, corr_ref,
-):
-    rows = q_ref.shape[0]
-    total = kv_ref.shape[0]
-    width = HEAD_WIDTH
-    block = KEY_BLOCK
+    weights_qb.finish()
     scale = width ** (-0.5)
-    start_row = bound_ref[0:1, :]
-    end_row = bound_ref[1:2, :]
-    low = (jnp.min(start_row) * (1.0 / ALIGN)).astype(jnp.int32) * ALIGN
-    high = jnp.max(end_row).astype(jnp.int32)
-    steps = lax.div(high - low + (block - 1), block)
-    for g in range(QUERY_PER_KEY):
-        query = q_ref[:, g * width : (g + 1) * width]
-        q4_ref[g] = query
-        q4t_ref[g] = query.T
+    half_rows = local // 2
+    start_row, end_row = bound_ref[0:1, :], bound_ref[1:2, :]
     num_ref[...] = jnp.zeros_like(num_ref)
     den_ref[...] = jnp.zeros_like(den_ref)
     dq_ref[...] = jnp.zeros_like(dq_ref)
-    dkv_ref[...] = jnp.zeros_like(dkv_ref)
-
-    def rows_of(i):
-        wanted = low + i * block
-        first = jnp.minimum(wanted, total - block)
-        return wanted, first, pl.ds(pl.multiple_of(first, ALIGN), block)
-
-    def forward(i, carry):
-        wanted, first, at = rows_of(i)
-        key = kv_ref[at, 0:width]
-        value = kv_ref[at, width : 2 * width]
-        place = (lax.broadcasted_iota(jnp.int32, (block, rows), 0) + first).astype(jnp.float32)
-        floor_row = jnp.maximum(start_row, wanted.astype(jnp.float32))
-        mask = (place >= floor_row) & (place < end_row)
+
+    def pieces(half, offset):
+        across = wrap(torus.place["y"] + offset) * SIDE * (1 - half)
+        base = across + wrap(torus.place["x"] + offset) * half
+        stride = 1 + (SIDE - 1) * half
+        return [
+            pl.multiple_of((base + i * stride) * local + half * half_rows, half_rows)
+            for i in range(SIDE)
+        ]
+
+    def both_halves(step, offset):
+        def body(half, carry):
+            step(half, offset)
+            return carry
+
+        lax.fori_loop(0, 2, body, 0)
+
+    def key_rows(starts):
+        parts = [kv_ref[pl.ds(start, half_rows), :] for start in starts]
+        both = jnp.concatenate(parts, axis=0)
+        return both[:, 0:width], both[:, width:]
+
+    def slot_of(half, offset):
+        return half * SIDE + offset % SIDE
+
+    def forward(half, offset):
+        starts = pieces(half, offset)
+        key, value = key_rows(starts)
+        line = lax.broadcasted_iota(jnp.int32, (half_rows, local), 0)
+        place = jnp.concatenate([line + start for start in starts], axis=0).astype(jnp.float32)
+        mask = (place >= start_row) & (place < end_row)
         for g in range(QUERY_PER_KEY):
             scores = jnp.dot(key, q4t_ref[g], preferred_element_type=jnp.float32)
             exponent = jnp.where(mask, jnp.exp2(scores * (scale * LOG2E)), 0.0)
-            den_ref[g] += jnp.sum(exponent.reshape(block // 8, 8, rows), axis=0)
+            den_ref[g] += jnp.sum(exponent.reshape(SIDE * half_rows // 8, 8, local), axis=0)
             rounded = exponent.astype(jnp.bfloat16)
-            exp_ref[g, pl.ds(pl.multiple_of(i * block, block), block), :] = rounded
-            num_ref[g] += lax.dot_general(
-                rounded, value, TN, preferred_element_type=jnp.float32
+            exp_ref[slot_of(half, offset), g] = rounded
+            num_ref[g] += lax.dot_general(rounded, value, TN, preferred_element_type=jnp.float32)
+
+    def backward(half, offset):
+        starts = pieces(half, offset)
+        key, value = key_rows(starts)
+        dk = jnp.zeros((SIDE * half_rows, width), jnp.float32)
+        dv = jnp.zeros((SIDE * half_rows, width), jnp.float32)
+        for g in range(QUERY_PER_KEY):
+            grads = jnp.dot(value, up4t_ref[g], preferred_element_type=jnp.float32)
+            rounded = exp_ref[slot_of(half, offset), g]
+            ds = (rounded.astype(jnp.float32) * (grads - corr_ref[g])).astype(jnp.bfloat16)
+            dk += jnp.dot(ds, q4_ref[g], preferred_element_type=jnp.float32)
+            dv += jnp.dot(rounded, up4_ref[g], preferred_element_type=jnp.float32)
+            dq_ref[:, g * width : (g + 1) * width] += lax.dot_general(
+                ds, key, TN, preferred_element_type=jnp.float32
             )
-        return carry
-
-    lax.fori_loop(0, steps, forward, 0)
+        for i, start in enumerate(starts):
+            rows_here = slice(i * half_rows, (i + 1) * half_rows)
+            at = pl.ds(start, half_rows)
+            dkv_ref[at, 0:width] = (dk[rows_here] * scale).astype(jnp.bfloat16)
+            dkv_ref[at, width:] = dv[rows_here].astype(jnp.bfloat16)
+
+    keys_values.far()
+    query_heads(wqb_ref, (2, 3))
+    keys_values.cross((0, -1))
+    both_halves(forward, 0)
+    keys_values.cross((1, 2))
+    both_halves(forward, -1)
+    both_halves(forward, 1)
+    keys_values.finish()
+    both_halves(forward, 2)
+
     for g in range(QUERY_PER_KEY):
         columns = slice(g * width, (g + 1) * width)
         inverse = 1.0 / jnp.sum(den_ref[g].T, axis=1, keepdims=True)
@@ -507,112 +494,46 @@
         product = up.astype(jnp.float32) * context.astype(jnp.float32)
         corr_ref[g] = jnp.sum(product.T, axis=0, keepdims=True)
 
-    def backward(i, carry):
-        wanted, first, at = rows_of(i)
-        key = kv_ref[at, 0:width]
-        value = kv_ref[at, width : 2 * width]
-        dk = jnp.zeros((block, width), jnp.float32)
-        dv = jnp.zeros((block, width), jnp.float32)
-        for g in range(QUERY_PER_KEY):
-            grads = jnp.dot(value, up4t_ref[g], preferred_element_type=jnp.float32)
-            rounded = exp_ref[g, pl.ds(pl.multiple_of(i * block, block), block), :]
-            ds = (rounded.astype(jnp.float32) * (grads - corr_ref[g])).astype(jnp.bfloat16)
-            dk += jnp.dot(ds, q4_ref[g], preferred_element_type=jnp.float32)
-            dv += jnp.dot(rounded, up4_ref[g], preferred_element_type=jnp.float32)
-            dq_ref[:, g * width : (g + 1) * width] += lax.dot_general(
-                ds, key, TN, preferred_element_type=jnp.float32
-            )
-        kept = dkv_ref[at, :].astype(jnp.float32)
-        dkv_ref[at, 0:width] = (kept[:, 0:width] + dk * scale).astype(jnp.bfloat16)
-        dkv_ref[at, width : 2 * width] = (kept[:, width:] + dv).astype(jnp.bfloat16)
-        return carry
-
-    lax.fori_loop(0, steps, backward, 0)
-    dq_ref[...] = dq_ref[...] * scale
-
-
-def attention(queries, keys_values, upstream, bounds):
-    rows = queries.shape[0]
-    total = keys_values.shape[0]
-    group = QUERY_PER_KEY
-    width = HEAD_WIDTH
-    vmem = pl.BlockSpec(memory_space=pltpu.VMEM)
-    bf16, f32 = jnp.bfloat16, jnp.float32
-    return pl.pallas_call(
-        attention_kernel,
-        out_shape=(
-            jax.ShapeDtypeStruct((rows, group * width), bf16),
-            jax.ShapeDtypeStruct((rows, group * width), f32),
-            jax.ShapeDtypeStruct((total, 2 * width), bf16),
-        ),
-        in_specs=[vmem] * 4,
-        out_specs=(vmem, vmem, vmem),
-        scratch_shapes=[
-            pltpu.VMEM((group, total + KEY_BLOCK, rows), bf16),
-            pltpu.VMEM((group, rows, width), bf16),
-            pltpu.VMEM((group, width, rows), bf16),
-            pltpu.VMEM((group, rows, width), bf16),
-            pltpu.VMEM((group, width, rows), bf16),
-            pltpu.VMEM((group, rows, width), f32),
-            pltpu.VMEM((group, 8, rows), f32),
-            pltpu.VMEM((group, 1, rows), f32),
-        ],
-        compiler_params=pltpu.CompilerParams(vmem_limit_bytes=28 * 1024 * 1024),
-        cost_estimate=pl.CostEstimate(
-            flops=14 * group * rows * total * width,
-            bytes_accessed=8 * total * width,
-            transcendentals=group * rows * total,
-        ),
-    )(queries, keys_values, upstream, bounds)
-
-
-def gradient_kernel(
-    dq_ref, dkv_in_ref, raw_ref, normed_ref, wq_ref, wkv_ref, rope_ref, tokens_ref,
-    norm_gain_ref, query_gain_ref, key_gain_ref,
-    token_grads_ref, projection_grads_ref, gains_ref,
-    send_sems, recv_sems, local_sems,
-    dkv_ref, jq_ref, jkv_ref, gq_ref, gkv_ref, dkv_sum_ref,
-    terms_ref, pair_ref, zfar_ref, znear_ref, gx_ref, gy_ref, gz_ref, gc_ref,
-    *boxes,
-):
-    width = HEAD_WIDTH
-    split = QUERY_PER_KEY * width
-    torus = Torus(send_sems, recv_sems)
-    load = pltpu.make_async_copy(dkv_in_ref, dkv_ref, local_sems.at[0])
-    load.start()
-    torus.greet((1, 2, 3))
     dkv = Scatter(torus, dkv_ref, *boxes[0:4])
     dwq = Scatter(torus, gq_ref, *boxes[4:8])
     dwkv = Scatter(torus, gkv_ref, *boxes[8:12])
-    dkv.start(dkv_in_ref)
-
-    cosine, sine = rope_ref[0], rope_ref[1]
+    both_halves(backward, 2)
+    dkv.start()
+    for offset in (1, -1):
+        both_halves(backward, offset)
+        dkv.turn(steps=(offset,))
+    both_halves(backward, 0)
+    dkv.land()
+
     query_gain_grads = jnp.zeros((1, width), jnp.float32)
     for g in range(QUERY_PER_KEY):
         columns = slice(g * width, (g + 1) * width)
         raw_grads, gain_grads = head_map_back(
-            raw_ref[:, columns], query_gain_ref[...], cosine, sine, dq_ref[:, columns]
+            raw_ref[:, columns], query_gain_ref[...], cosine, sine, dq_ref[:, columns] * scale
         )
         jq_ref[:, columns] = raw_grads.astype(jnp.bfloat16)
         query_gain_grads = query_gain_grads + gain_grads
-    load.wait()
-    dkv.turn()
 
     def weight_grads(j_ref, g_ref):
-        def body(i, carry):
-            at = pl.ds(pl.multiple_of(i * 256, 256), 256)
-            g_ref[at, :] = lax.dot_general(
-                normed_ref[:, at], j_ref[...], TN, preferred_element_type=jnp.float32
-            ).astype(jnp.bfloat16)
-            return carry
-
-        lax.fori_loop(0, normed_ref.shape[1] // 256, body, 0)
-
-    weight_grads(jq_ref, gq_ref)
+        def piece(half, offset):
+            starts = pieces(half, offset)
+            rows = jnp.concatenate(
+                [normed_ref[:, pl.ds(start, half_rows)] for start in starts], axis=1
+            )
+            grads = lax.dot_general(rows, j_ref[...], TN, preferred_element_type=jnp.float32)
+            for i, start in enumerate(starts):
+                g_ref[pl.ds(start, half_rows), :] = grads[
+                    i * half_rows : (i + 1) * half_rows
+                ].astype(jnp.bfloat16)
+
+        return piece
+
+    query_weights = weight_grads(jq_ref, gq_ref)
+    both_halves(query_weights, 2)
     dwq.start()
-    dkv.land()
     dkv.turn_two()
-    dwq.turn((2, 1))
+    for offset in (1, -1, 0):
+        both_halves(query_weights, offset)
 
     def keep_dkv(at, total):
         dkv_sum_ref[at, :] = total
@@ -623,21 +544,27 @@
     )
     jkv_ref[:, :width] = raw_grads.astype(jnp.bfloat16)
     jkv_ref[:, width:] = dkv_sum_ref[:, width:].astype(jnp.bfloat16)
-    weight_grads(jkv_ref, gkv_ref)
+    pair_weights = weight_grads(jkv_ref, gkv_ref)
+    both_halves(pair_weights, 2)
     dwkv.start()
-    dwq.turn((-1, 0))
+    dwq.turn()
+    for offset in (1, -1, 0):
+        both_halves(pair_weights, offset)
 
     def input_terms(i, carry):
         at = pl.ds(pl.multiple_of(i * 256, 256), 256)
         terms_ref[:, at] = (
-            lax.dot_general(jq_ref[...], wq_ref[at, :], NT, preferred_element_type=jnp.float32)
+            lax.dot_general(
+                jq_ref[:, 0:pair_width], wqa_ref[at, :], NT, preferred_element_type=jnp.float32
+            )
+            + lax.dot_general(
+                jq_ref[:, pair_width:], wqb_ref[at, :], NT, preferred_element_type=jnp.float32
+            )
             + lax.dot_general(jkv_ref[...], wkv_ref[at, :], NT, preferred_element_type=jnp.float32)
         ).astype(jnp.bfloat16)
         return carry
 
     lax.fori_loop(0, terms_ref.shape[1] // 256, input_terms, 0)
-
-    count = tokens_ref.shape[0]
 
     def term_rows(step, part=None, flip=False):
         core = torus.place["core"]
@@ -650,17 +577,14 @@
         step: torus.send(term_rows(step, flip=True), pair_ref.at[step % SIDE], "core", 1)
         for step in (2, 1, -1, 0)
     }
-    dwq.land((2,))
-    dwkv.turn((2,))
-    far = {}
     torus.arrive(pair[2], pair_ref.at[2])
     add_to(term_rows(2), pair_ref.at[2])
+    far = {}
     for step in (1, -1):
         far[step] = torus.send(
             term_rows(2, part_of(step)), zfar_ref.at[part_of(step)], "z", step
         )
-    dwq.land((1, -1))
-    dwq.turn_two()
+    dwkv.turn()
     near = {}
     for step in (1, -1):
         torus.arrive(pair[step], pair_ref.at[step % SIDE])
@@ -668,8 +592,8 @@
         torus.arrive(far[step], zfar_ref.at[part_of(step)])
         add_to(term_rows(step, part_of(step)), zfar_ref.at[part_of(step)])
         near[step] = torus.send(term_rows(step), znear_ref.at[part_of(step)], "z", step)
-    dwkv.turn((1, -1, 0))
-    dwq.land((0,))
+    dwq.land((2, 1, -1))
+    dwq.turn_two()
     torus.arrive(pair[0], pair_ref.at[0])
     for step in (1, -1):
         torus.arrive(near[step], znear_ref.at[part_of(step)])
@@ -715,48 +639,73 @@
         projection_grads_ref[at, split:] = total
 
     sent = share("z", gz_ref)
-    dwkv.land((2, 1))
+    dwq.land((0,))
     collect("z", gz_ref, sent)
     sent = share("core", gc_ref)
-    dwkv.land((-1,))
+    dwkv.land((2, 1))
     collect("core", gc_ref, sent)
     sent = share("x", gx_ref)
+    dwkv.land((-1,))
     dwkv.turn_two()
-    dwq.finish(keep_q)
     collect("x", gx_ref, sent)
     sent = share("y", gy_ref)
     dwkv.land((0,))
+    dwq.finish(keep_q)
+    collect("y", gy_ref, sent)
     dwkv.finish(keep_kv)
-    collect("y", gy_ref, sent)
     torus.close()
 
 
-def gradients(
-    dq, dkv, raw, normed, wq, wkv, rope, tokens, norm_gain, query_gain, key_gain
-):
-    local, depth = normed.shape
-    count = tokens.shape[0]
-    total = dkv.shape[0]
-    width = HEAD_WIDTH
-    split = QUERY_PER_KEY * width
-    rows = depth // (SIDE * SIDE)
+def layer(tokens, shard, norm_gain, query_gain, key_gain, segments, waves, upstream):
+    rows, columns = shard.shape
+    count, depth = tokens.shape
+    local = upstream.shape[0]
+    total = local * SIDE * SIDE
+    group, width = QUERY_PER_KEY, HEAD_WIDTH
+    split = group * width
     gains = (depth // width + 8, width)
+    copies = 7 * 40 + 8 + 8 + 10
+    bf16, f32 = jnp.bfloat16, jnp.float32
     vmem = pl.BlockSpec(memory_space=pltpu.VMEM)
-    copies = 3 * 40 + 8 + 10
-    bf16, f32 = jnp.bfloat16, jnp.float32
+    hbm = pl.BlockSpec(memory_space=pltpu.HBM)
     return pl.pallas_call(
-        gradient_kernel,
+        layer_kernel,
         out_shape=(
+            jax.ShapeDtypeStruct((local, split), bf16),
             jax.ShapeDtypeStruct((count, depth), f32),
-            jax.ShapeDtypeStruct((rows, split + 2 * width), f32),
+            jax.ShapeDtypeStruct((rows, columns), f32),
             jax.ShapeDtypeStruct(gains, f32),
         ),
-        in_specs=[vmem] * 11,
-        out_specs=(vmem,) * 3,
+        in_specs=[hbm] * 8,
+        out_specs=(vmem,) * 4,
         scratch_shapes=[
             pltpu.SemaphoreType.DMA((copies,)),
             pltpu.SemaphoreType.DMA((copies,)),
-            pltpu.SemaphoreType.DMA((1,)),
+            pltpu.SemaphoreType.DMA((10,)),
+            pltpu.VMEM(tokens.shape, bf16),
+            pltpu.VMEM(norm_gain.shape, f32),
+            pltpu.VMEM(query_gain.shape, f32),
+            pltpu.VMEM(key_gain.shape, f32),
+            pltpu.VMEM(segments.shape, jnp.int32),
+            pltpu.VMEM(waves.shape, f32),
+            pltpu.VMEM(upstream.shape, bf16),
+            pltpu.VMEM((total, 2 * width), bf16),
+            pltpu.VMEM((local, split + width), f32),
+            pltpu.VMEM((local, depth), bf16),
+            pltpu.VMEM((depth, 2 * width), bf16),
+            pltpu.VMEM((depth, split // 2), bf16),
+            pltpu.VMEM((depth, split // 2), bf16),
+            pltpu.VMEM((2, local, width), f32),
+            pltpu.VMEM((2, local), f32),
+            pltpu.VMEM((2 * SIDE, group, total // (2 * SIDE), local), bf16),
+            pltpu.VMEM((group, local, width), bf16),
+            pltpu.VMEM((group, width, local), bf16),
+            pltpu.VMEM((group, local, width), bf16),
+            pltpu.VMEM((group, width, local), bf16),
+            pltpu.VMEM((group, local, width), f32),
+            pltpu.VMEM((group, 8, local), f32),
+            pltpu.VMEM((group, 1, local), f32),
+            pltpu.VMEM((local, split), f32),
             pltpu.VMEM((total, 2 * width), bf16),
             pltpu.VMEM((local, split), bf16),
             pltpu.VMEM((local, 2 * width), bf16),
@@ -772,59 +721,70 @@
             pltpu.VMEM((SIDE,) + gains, f32),
             pltpu.VMEM((2,) + gains, f32),
         ]
-        + scatter_scratch(total // (SIDE * SIDE), 2 * width)
+        + scatter_scratch(local, 2 * width)
         + scatter_scratch(rows, split)
         + scatter_scratch(rows, 2 * width),
         compiler_params=pltpu.CompilerParams(
-            collective_id=1, has_side_effects=True, vmem_limit_bytes=40 * 1024 * 1024
+            collective_id=0, has_side_effects=True, vmem_limit_bytes=60 * 1024 * 1024
         ),
         cost_estimate=pl.CostEstimate(
-            flops=4 * local * depth * (split + 2 * width),
-            bytes_accessed=4 * depth * (split + 2 * width),
-            transcendentals=0,
+            flops=6 * local * depth * columns + 14 * group * local * total * width,
+            bytes_accessed=8 * depth * columns,
+            transcendentals=group * local * total,
         ),
-    )(dq, dkv, raw, normed, wq, wkv, rope, tokens, norm_gain, query_gain, key_gain)
+    )(tokens, shard, norm_gain, query_gain, key_gain, segments, waves, upstream)
 
 
 def finish_kernel(
-    token_ref, projection_ref, gains_ref,
-    token_out, projection_out, norm_out, query_out, key_out,
-    sems,
+    context_ref, token_ref, projection_ref, gains_ref,
+    context_out, token_out, projection_out, norm_out, query_out, key_out,
+    context_box, token_box, projection_box, gains_box, sems,
 ):
-    copies = [
-        pltpu.make_async_copy(token_ref, token_out, sems.at[0]),
-        pltpu.make_async_copy(projection_ref, projection_out, sems.at[1]),
-    ]
-    for copy in copies:
-        copy.start()
+    loads, stores = [], []
+    for i, (source, box, target) in enumerate(
+        (
+            (gains_ref, gains_box, None),
+            (projection_ref, projection_box, projection_out),
+            (token_ref, token_box, token_out),
+            (context_ref, context_box, context_out),
+        )
+    ):
+        loads.append(pltpu.make_async_copy(source, box, sems.at[2 * i]))
+        if target is not None:
+            stores.append(pltpu.make_async_copy(box, target, sems.at[2 * i + 1]))
+        loads[-1].start()
+    loads[0].wait()
     lines = norm_out.shape[0]
-    norm_out[...] = gains_ref[0:lines, :]
-    query_out[...] = gains_ref[lines : lines + 1, :]
-    key_out[...] = gains_ref[lines + 1 : lines + 2, :]
-    for copy in copies:
-        copy.wait()
-
-
-def finish(token_grads, projection_grads, gains):
+    norm_out[...] = gains_box[0:lines, :]
+    query_out[...] = gains_box[lines : lines + 1, :]
+    key_out[...] = gains_box[lines + 1 : lines + 2, :]
+    for load, store in zip(loads[1:], stores):
+        load.wait()
+        store.start()
+    for store in stores:
+        store.wait()
+
+
+def finish(context, token_grads, projection_grads, gains):
     width = HEAD_WIDTH
     vmem = pl.BlockSpec(memory_space=pltpu.VMEM)
     hbm = pl.BlockSpec(memory_space=pltpu.HBM)
-    anywhere = pl.BlockSpec(memory_space=pl.ANY)
     f32 = jnp.float32
+    arrays = (context, token_grads, projection_grads)
     return pl.pallas_call(
         finish_kernel,
-        out_shape=(
-            jax.ShapeDtypeStruct(token_grads.shape, f32),
-            jax.ShapeDtypeStruct(projection_grads.shape, f32),
+        out_shape=tuple(jax.ShapeDtypeStruct(array.shape, array.dtype) for array in arrays)
+        + (
             jax.ShapeDtypeStruct((token_grads.shape[1] // width, width), f32),
             jax.ShapeDtypeStruct((1, width), f32),
             jax.ShapeDtypeStruct((1, width), f32),
         ),
-        in_specs=[anywhere, anywhere, vmem],
-        out_specs=(hbm, hbm, vmem, vmem, vmem),
-        scratch_shapes=[pltpu.SemaphoreType.DMA((2,))],
-        compiler_params=pltpu.CompilerParams(vmem_limit_bytes=4 * 1024 * 1024),
-    )(token_grads, projection_grads, gains)
+        in_specs=[hbm] * 4,
+        out_specs=(hbm,) * 3 + (vmem,) * 3,
+        scratch_shapes=[pltpu.VMEM(array.shape, array.dtype) for array in arrays + (gains,)]
+        + [pltpu.SemaphoreType.DMA((8,))],
+        compiler_params=pltpu.CompilerParams(vmem_limit_bytes=60 * 1024 * 1024),
+    )(*arrays, gains)
 
 
 def rope_waves(local, blocks, width):
@@ -845,15 +805,11 @@
     query_gain = query_gain.reshape(1, -1)
     key_gain = key_gain.reshape(1, -1)
     segments = segment_ids.reshape(-1, 128)
-    queries, keys_values, raw, normed, wkv, wq, rope, bounds = project(
-        tokens, projection, norm_gain, query_gain, key_gain, segments, waves
-    )
-    context, query_grads, kv_grads = attention(queries, keys_values, context_cotangent, bounds)
-    token_grads, projection_grads, gains = gradients(
-        query_grads, kv_grads, raw, normed, wq, wkv, rope, tokens, norm_gain, query_gain, key_gain
-    )
-    token_grads, projection_grads, norm_gains, query_gains, key_gains = finish(
-        token_grads, projection_grads, gains
+    context, token_grads, projection_grads, gains = layer(
+        tokens, projection, norm_gain, query_gain, key_gain, segments, waves, context_cotangent
+    )
+    context, token_grads, projection_grads, norm_gains, query_gains, key_gains = finish(
+        context, token_grads, projection_grads, gains
     )
     return (
         context,

time: 148 us -> 136 us (0.919)
  Pallas kernels: 142 us -> 135 us
  local copies, waits for them, and re-layouts: 5.67 us -> 0 us
    pallas_call x4 -> x2, Pallas kernels: 142 us -> 135 us  [the longest x1 132 us: layer(): pl.pallas_call(layer_kernel, out_shape=(jax.ShapeDtypeStruct((local, spli...]
    unnamed x24 -> x0, local copies, waits for them, and re-layouts: 5.67 us -> none
where the time goes in v4:
time: 136 us
  Pallas kernels  135 us (99%)
    pallas_call x1, Pallas kernels, layer(): pl.pallas_call(layer_kernel, out_shape=(jax.ShapeDtypeStruct((local, spli...  132 us
    pallas_call x1, Pallas kernels, finish(): pl.pallas_call(finish_kernel, out_shape=tuple((jax.ShapeDtypeStruct(array...  2.97 us

profile of v4, /device:TPU:1, one launch (start us, length us, event | category | flops | bytes accessed | tf_op | source)
XLA Modules:
  0.0 136.1 jit_solution(9613990526737835421)
XLA Ops:
  0.6 132.3 %shard_map.127 = (bf16[256,512]{1,0:T(8,128)(2,1)}, f32[32,4096]{1,0:T(8,128)}, f32[256,768]{1,0:T(8,128)}, f32[40,128]{1,0:T(8,128)}) custom-call(bf16[32,4096]{1,0:T(8,128)(2,1)} %tokens_hbm.1, bf16[256,768]{1,0:T(8,128)(2,1)} %shard_hbm.1, f32[1,4096]{1,0:T(1,128)} %bitcast.7, f32[1,128]{1,0:T(1,128)} %bitcast.10, f32[1,128]{1,0:T(1,128)} %bitcast.11, ...), custom_call_target="tpu_custom_call" | custom-call | flops 12348030976 | bytes 25165824 | tf_op jit(solution)/shard_map/pallas_call | solution.py:671
  132.9 3.0 %shard_map.128 = (bf16[256,512]{1,0:T(8,128)(2,1)}, f32[32,4096]{1,0:T(8,128)}, f32[256,768]{1,0:T(8,128)}, f32[32,128]{1,0:T(8,128)}, f32[1,128]{1,0:T(1,128)}, /*index=5*/f32[1,128]{1,0:T(1,128)}) custom-call(bf16[256,512]{1,0:T(8,128)(2,1)} %get-tuple-element.16.context_ref, f32[32,4096]{1,0:T(8,128)} %get-tuple-element.17.token_ref, ...), custom_call_target="tpu_custom_call" | custom-call | tf_op jit(solution)/shard_map/pallas_call | solution.py:774

commit v5 on v4

--- a/solution.py
+++ b/solution.py
@@ -331,9 +331,11 @@
     pair = {0: torus.send(mine, mine, "core", 1)}
 
     loads[3].wait()
+    weights_kv.start()
     weights_qa.near()
-    weights_kv.start()
-    for load in loads[4:]:
+    loads[4].wait()
+    weights_qb.start()
+    for load in loads[5:]:
         load.wait()
     local = rope_ref.shape[1]
     near_cosine, near_sine = waves_ref[0:local, :], waves_ref[local : 2 * local, :]
@@ -358,7 +360,6 @@
     weights_qa.cross((0, -1, 1))
     weights_kv.near()
     weights_qa.cross((2,))
-    weights_qb.start()
 
     segments = segments_ref[...]
     lines = local // segments.shape[1]
@@ -390,11 +391,10 @@
             q4_ref[g] = query
             q4t_ref[g] = query.T
 
-    weights_kv.cross((0, -1))
-    query_heads(wqa_ref, (0, 1))
-    weights_kv.cross((1,))
+    weights_kv.cross((0, -1, 1))
     weights_qb.near()
     weights_kv.cross((2,))
+    query_heads(wqa_ref, (0, 1))
     weights_qb.far()
     weights_kv.finish()
     raw = jnp.dot(normed_ref[...], wkv_ref[...], preferred_element_type=jnp.float32)
@@ -535,23 +535,7 @@
     for offset in (1, -1, 0):
         both_halves(query_weights, offset)
 
-    def keep_dkv(at, total):
-        dkv_sum_ref[at, :] = total
-
-    dkv.finish(keep_dkv)
-    raw_grads, key_gain_grads = head_map_back(
-        raw_ref[:, split:], key_gain_ref[...], cosine, sine, dkv_sum_ref[:, :width]
-    )
-    jkv_ref[:, :width] = raw_grads.astype(jnp.bfloat16)
-    jkv_ref[:, width:] = dkv_sum_ref[:, width:].astype(jnp.bfloat16)
-    pair_weights = weight_grads(jkv_ref, gkv_ref)
-    both_halves(pair_weights, 2)
-    dwkv.start()
-    dwq.turn()
-    for offset in (1, -1, 0):
-        both_halves(pair_weights, offset)
-
-    def input_terms(i, carry):
+    def query_terms(i, carry):
         at = pl.ds(pl.multiple_of(i * 256, 256), 256)
         terms_ref[:, at] = (
             lax.dot_general(
@@ -560,11 +544,31 @@
             + lax.dot_general(
                 jq_ref[:, pair_width:], wqb_ref[at, :], NT, preferred_element_type=jnp.float32
             )
+        ).astype(jnp.bfloat16)
+        return carry
+
+    lax.fori_loop(0, terms_ref.shape[1] // 256, query_terms, 0)
+
+    def keep_dkv(at, total):
+        dkv_sum_ref[at, :] = total
+
+    dkv.finish(keep_dkv)
+    raw_grads, key_gain_grads = head_map_back(
+        raw_ref[:, split:], key_gain_ref[...], cosine, sine, dkv_sum_ref[:, :width]
+    )
+    jkv_ref[:, :width] = raw_grads.astype(jnp.bfloat16)
+    jkv_ref[:, width:] = dkv_sum_ref[:, width:].astype(jnp.bfloat16)
+    pair_weights = weight_grads(jkv_ref, gkv_ref)
+    both_halves(pair_weights, 2)
+    dwkv.start()
+
+    def value_terms(i, carry):
+        at = pl.ds(pl.multiple_of(i * 256, 256), 256)
+        terms_ref[:, at] = (
+            terms_ref[:, at].astype(jnp.float32)
             + lax.dot_general(jkv_ref[...], wkv_ref[at, :], NT, preferred_element_type=jnp.float32)
         ).astype(jnp.bfloat16)
         return carry
-
-    lax.fori_loop(0, terms_ref.shape[1] // 256, input_terms, 0)
 
     def term_rows(step, part=None, flip=False):
         core = torus.place["core"]
@@ -573,10 +577,15 @@
         start = index * count + (0 if part is None else part * (count // 2))
         return terms_ref.at[pl.ds(pl.multiple_of(start, count // 2), size), :]
 
+    dwq.turn((2, 1))
+    lax.fori_loop(0, terms_ref.shape[1] // 256, value_terms, 0)
     pair = {
         step: torus.send(term_rows(step, flip=True), pair_ref.at[step % SIDE], "core", 1)
         for step in (2, 1, -1, 0)
     }
+    dwq.turn((-1, 0))
+    for offset in (1, -1, 0):
+        both_halves(pair_weights, offset)
     torus.arrive(pair[2], pair_ref.at[2])
     add_to(term_rows(2), pair_ref.at[2])
     far = {}
@@ -585,14 +594,16 @@
             term_rows(2, part_of(step)), zfar_ref.at[part_of(step)], "z", step
         )
     dwkv.turn()
-    near = {}
     for step in (1, -1):
         torus.arrive(pair[step], pair_ref.at[step % SIDE])
         add_to(term_rows(step), pair_ref.at[step % SIDE])
+    dwq.land((2,))
+    near = {}
+    for step in (1, -1):
         torus.arrive(far[step], zfar_ref.at[part_of(step)])
         add_to(term_rows(step, part_of(step)), zfar_ref.at[part_of(step)])
         near[step] = torus.send(term_rows(step), znear_ref.at[part_of(step)], "z", step)
-    dwq.land((2, 1, -1))
+    dwq.land((1, -1))
     dwq.turn_two()
     torus.arrive(pair[0], pair_ref.at[0])
     for step in (1, -1):
@@ -640,19 +651,19 @@
 
     sent = share("z", gz_ref)
     dwq.land((0,))
+    dwkv.land((2,))
     collect("z", gz_ref, sent)
     sent = share("core", gc_ref)
-    dwkv.land((2, 1))
+    dwkv.land((1, -1))
     collect("core", gc_ref, sent)
     sent = share("x", gx_ref)
-    dwkv.land((-1,))
     dwkv.turn_two()
     collect("x", gx_ref, sent)
     sent = share("y", gy_ref)
+    dwq.finish(keep_q)
     dwkv.land((0,))
-    dwq.finish(keep_q)
+    dwkv.finish(keep_kv)
     collect("y", gy_ref, sent)
-    dwkv.finish(keep_kv)
     torus.close()
 
 

time: 136 us -> 133 us (0.978)
  Pallas kernels: 135 us -> 132 us
    pallas_call x1, Pallas kernels: 132 us -> 129 us  [layer(): pl.pallas_call(layer_kernel, out_shape=(jax.ShapeDtypeStruct((local, spli...]
where the time goes in v5:
time: 133 us; the launch traced here: 132 us
  Pallas kernels  132 us (99%)
    pallas_call x1, Pallas kernels, layer(): pl.pallas_call(layer_kernel, out_shape=(jax.ShapeDtypeStruct((local, spli...  129 us
    pallas_call x1, Pallas kernels, finish(): pl.pallas_call(finish_kernel, out_shape=tuple((jax.ShapeDtypeStruct(array...  2.97 us

profile of v5, /device:TPU:1, one launch (start us, length us, event | category | flops | bytes accessed | tf_op | source)
XLA Modules:
  0.0 132.4 jit_solution(4368812446039506219)
XLA Ops:
  0.6 128.6 %shard_map.127 = (bf16[256,512]{1,0:T(8,128)(2,1)}, f32[32,4096]{1,0:T(8,128)}, f32[256,768]{1,0:T(8,128)}, f32[40,128]{1,0:T(8,128)}) custom-call(bf16[32,4096]{1,0:T(8,128)(2,1)} %tokens_hbm.1, bf16[256,768]{1,0:T(8,128)(2,1)} %shard_hbm.1, f32[1,4096]{1,0:T(1,128)} %bitcast.7, f32[1,128]{1,0:T(1,128)} %bitcast.10, f32[1,128]{1,0:T(1,128)} %bitcast.11, ...), custom_call_target="tpu_custom_call" | custom-call | flops 12348030976 | bytes 25165824 | tf_op jit(solution)/shard_map/pallas_call | solution.py:682
  129.3 3.0 %shard_map.128 = (bf16[256,512]{1,0:T(8,128)(2,1)}, f32[32,4096]{1,0:T(8,128)}, f32[256,768]{1,0:T(8,128)}, f32[32,128]{1,0:T(8,128)}, f32[1,128]{1,0:T(1,128)}, /*index=5*/f32[1,128]{1,0:T(1,128)}) custom-call(bf16[256,512]{1,0:T(8,128)(2,1)} %get-tuple-element.16.context_ref, f32[32,4096]{1,0:T(8,128)} %get-tuple-element.17.token_ref, ...), custom_call_target="tpu_custom_call" | custom-call | tf_op jit(solution)/shard_map/pallas_call | solution.py:785

commit v6 on v5

--- a/solution.py
+++ b/solution.py
@@ -416,6 +416,8 @@
     dq_ref[...] = jnp.zeros_like(dq_ref)
 
     def pieces(half, offset):
+        if half is None:
+            return pieces(0, offset) + pieces(1, offset)
         across = wrap(torus.place["y"] + offset) * SIDE * (1 - half)
         base = across + wrap(torus.place["x"] + offset) * half
         stride = 1 + (SIDE - 1) * half
@@ -431,13 +433,20 @@
 
         lax.fori_loop(0, 2, body, 0)
 
+    def two_offsets(step, first):
+        def body(i, carry):
+            step(None, first - 2 * first * i)
+            return carry
+
+        lax.fori_loop(0, 2, body, 0)
+
     def key_rows(starts):
         parts = [kv_ref[pl.ds(start, half_rows), :] for start in starts]
         both = jnp.concatenate(parts, axis=0)
         return both[:, 0:width], both[:, width:]
 
-    def slot_of(half, offset):
-        return half * SIDE + offset % SIDE
+    def slots_of(half, offset):
+        return [side * SIDE + wrap(offset) for side in ((0, 1) if half is None else (half,))]
 
     def forward(half, offset):
         starts = pieces(half, offset)
@@ -448,19 +457,22 @@
         for g in range(QUERY_PER_KEY):
             scores = jnp.dot(key, q4t_ref[g], preferred_element_type=jnp.float32)
             exponent = jnp.where(mask, jnp.exp2(scores * (scale * LOG2E)), 0.0)
-            den_ref[g] += jnp.sum(exponent.reshape(SIDE * half_rows // 8, 8, local), axis=0)
+            den_ref[g] += jnp.sum(exponent.reshape(-1, 8, local), axis=0)
             rounded = exponent.astype(jnp.bfloat16)
-            exp_ref[slot_of(half, offset), g] = rounded
+            for i, slot in enumerate(slots_of(half, offset)):
+                exp_ref[slot, g] = rounded[i * SIDE * half_rows : (i + 1) * SIDE * half_rows]
             num_ref[g] += lax.dot_general(rounded, value, TN, preferred_element_type=jnp.float32)
 
     def backward(half, offset):
         starts = pieces(half, offset)
         key, value = key_rows(starts)
-        dk = jnp.zeros((SIDE * half_rows, width), jnp.float32)
-        dv = jnp.zeros((SIDE * half_rows, width), jnp.float32)
+        dk = jnp.zeros((len(starts) * half_rows, width), jnp.float32)
+        dv = jnp.zeros((len(starts) * half_rows, width), jnp.float32)
         for g in range(QUERY_PER_KEY):
             grads = jnp.dot(value, up4t_ref[g], preferred_element_type=jnp.float32)
-            rounded = exp_ref[slot_of(half, offset), g]
+            rounded = jnp.concatenate(
+                [exp_ref[slot, g] for slot in slots_of(half, offset)], axis=0
+            )
             ds = (rounded.astype(jnp.float32) * (grads - corr_ref[g])).astype(jnp.bfloat16)
             dk += jnp.dot(ds, q4_ref[g], preferred_element_type=jnp.float32)
             dv += jnp.dot(rounded, up4_ref[g], preferred_element_type=jnp.float32)
@@ -478,8 +490,7 @@
     keys_values.cross((0, -1))
     both_halves(forward, 0)
     keys_values.cross((1, 2))
-    both_halves(forward, -1)
-    both_halves(forward, 1)
+    two_offsets(forward, -1)
     keys_values.finish()
     both_halves(forward, 2)
 
@@ -499,9 +510,8 @@
     dwkv = Scatter(torus, gkv_ref, *boxes[8:12])
     both_halves(backward, 2)
     dkv.start()
-    for offset in (1, -1):
-        both_halves(backward, offset)
-        dkv.turn(steps=(offset,))
+    two_offsets(backward, 1)
+    dkv.turn()
     both_halves(backward, 0)
     dkv.land()
 

time: 133 us -> 128 us (0.962)
  Pallas kernels: 132 us -> 127 us
    pallas_call x1, Pallas kernels: 129 us -> 124 us  [layer(): pl.pallas_call(layer_kernel, out_shape=(jax.ShapeDtypeStruct((local, spli...]
where the time goes in v6:
time: 128 us
  Pallas kernels  127 us (99%)
    pallas_call x1, Pallas kernels, layer(): pl.pallas_call(layer_kernel, out_shape=(jax.ShapeDtypeStruct((local, spli...  124 us
    pallas_call x1, Pallas kernels, finish(): pl.pallas_call(finish_kernel, out_shape=tuple((jax.ShapeDtypeStruct(array...  2.97 us

profile of v6, /device:TPU:1, one launch (start us, length us, event | category | flops | bytes accessed | tf_op | source)
XLA Modules:
  0.0 127.9 jit_solution(9839067807293144383)
XLA Ops:
  0.6 124.1 %shard_map.127 = (bf16[256,512]{1,0:T(8,128)(2,1)}, f32[32,4096]{1,0:T(8,128)}, f32[256,768]{1,0:T(8,128)}, f32[40,128]{1,0:T(8,128)}) custom-call(bf16[32,4096]{1,0:T(8,128)(2,1)} %tokens_hbm.1, bf16[256,768]{1,0:T(8,128)(2,1)} %shard_hbm.1, f32[1,4096]{1,0:T(1,128)} %bitcast.7, f32[1,128]{1,0:T(1,128)} %bitcast.10, f32[1,128]{1,0:T(1,128)} %bitcast.11, ...), custom_call_target="tpu_custom_call" | custom-call | flops 12348030976 | bytes 25165824 | tf_op jit(solution)/shard_map/pallas_call | solution.py:692
  124.7 3.0 %shard_map.128 = (bf16[256,512]{1,0:T(8,128)(2,1)}, f32[32,4096]{1,0:T(8,128)}, f32[256,768]{1,0:T(8,128)}, f32[32,128]{1,0:T(8,128)}, f32[1,128]{1,0:T(1,128)}, /*index=5*/f32[1,128]{1,0:T(1,128)}) custom-call(bf16[256,512]{1,0:T(8,128)(2,1)} %get-tuple-element.16.context_ref, f32[32,4096]{1,0:T(8,128)} %get-tuple-element.17.token_ref, ...), custom_call_target="tpu_custom_call" | custom-call | tf_op jit(solution)/shard_map/pallas_call | solution.py:795
